TPU v7x, 256 devices: a whole 4x4x8 slice. The times are simulated.
256 devices in a mesh: dp: 8 (over x, z_lo), ctx: 32 (over z_hi, y, core).
Axes of the slice: x: 4, y: 4, z: 8 (z_hi: 4, z_lo: 2; z = z_hi * 2 + z_lo), core: 2. Of those that a mesh axis runs over, the one named last changes fastest.
Arguments:
- streams: bfloat16 [3, 32768, 4096], P(None, ('dp', 'ctx')), may hold values from -6 to 6
- out_grad: bfloat16 [32768, 4096], P(('dp', 'ctx')), may hold values from -6 to 6
- proj_weight: bfloat16 [4096, 4096], P('dp'), may hold values from -0.09375 to 0.09375
- long_filter: float32 [4096, 4096], P('dp', 'ctx'), may hold values from -0.09375 to 0.09375
- short_taps: float32 [3, 3, 4096], replicated, may hold values from -3 to 3
- doc_ids: int32 [32768], replicated, may hold values from 0 to 127, never falling along the last dimension, each value on 1 to 1024 neighbouring positions
Outputs:
- stream_grads: bfloat16 [3, 32768, 4096], P(None, ('dp', 'ctx'))
- proj_grad: float32 [4096, 4096], P(('dp', 'ctx'))
- filter_grad: float32 [4096, 4096], P('dp', 'ctx')
- tap_grad: float32 [3, 3, 4096], replicated
Inputs may be any that keep to these rules, and one draw needn't show every extreme that they name: `doc_ids`: never falls along the tokens; documents hold 1 to 1024 tokens and may cross device and sequence ends.
All inputs are finite; a program needn't handle non-finite values.
Results may differ from a plain program's by a relative error of at most 0.024.
Values may be sent and summed in bfloat16 or wider, within the bound.
A program may use at most 192 MiB of HBM per device.

v0:
```python
import math

import jax
import jax.numpy as jnp
from jax import lax
from jax.sharding import PartitionSpec as P


def from_behind(value, axis, by):
    peers = lax.axis_size(axis)
    pairs = [(i, i + by) for i in range(peers) if 0 <= i + by < peers]
    return lax.ppermute(value, axis, pairs)


def dft_table(length, sign, out_count, in_count):
    out_index = jnp.arange(out_count, dtype=jnp.int32)[:, None]
    in_index = jnp.arange(in_count, dtype=jnp.int32)[None, :]
    angle = (out_index * in_index % length).astype(jnp.float32) * (2.0 * math.pi / length)
    cosine = jnp.cos(angle)
    sine = sign * jnp.sin(angle)
    return jnp.stack([jnp.stack([cosine, -sine], 1), jnp.stack([sine, cosine], 1)], 0)


def transform(pair, total, sign, keep, parts):
    inputs, rows, width = pair.shape
    outer = 1 << (total.bit_length() - 1) // 2
    inner = total // outer
    used = rows // inner
    level = lax.Precision.HIGH
    blocks = pair.reshape(inputs, used, inner, width)
    first_table = dft_table(outer, sign, outer, used)[:, :, :inputs]
    first = jnp.einsum("pkqn,qnbc->pkbc", first_table, blocks, precision=level)
    outer_index = jnp.arange(outer, dtype=jnp.int32)[:, None]
    inner_index = jnp.arange(inner, dtype=jnp.int32)[None, :]
    angle = (outer_index * inner_index % total).astype(jnp.float32) * (2.0 * math.pi / total)
    twist_real = jnp.cos(angle)[:, :, None]
    twist_imag = (sign * jnp.sin(angle))[:, :, None]
    turned = jnp.stack(
        [
            first[0] * twist_real - first[1] * twist_imag,
            first[0] * twist_imag + first[1] * twist_real,
        ],
        0,
    )
    kept = keep // outer
    second_table = dft_table(inner, sign, kept, inner)[:parts]
    second = jnp.einsum("pkqn,qanc->pkac", second_table, turned, precision=level)
    return second.reshape(parts, keep, width)


def mirror_index(values):
    return jnp.roll(jnp.flip(values, 0), 1, 0)


def forward_spectra(product_chan, filter_full):
    length = product_chan.shape[0]
    total = 2 * length
    pair = jnp.stack([product_chan.astype(jnp.float32), filter_full], 0)
    spec = transform(pair, total, -1.0, total, 2)
    spec_real, spec_imag = (spec[0], spec[1])
    back_real = mirror_index(spec_real)
    back_imag = mirror_index(spec_imag)
    return (
        (spec_real + back_real) * 0.5,
        (spec_imag - back_imag) * 0.5,
        (spec_imag + back_imag) * 0.5,
        (back_real - spec_real) * 0.5,
    )


def apply_filter(spectra):
    prod_real, prod_imag, filt_real, filt_imag = spectra
    total = prod_real.shape[0]
    pair = jnp.stack(
        [
            prod_real * filt_real - prod_imag * filt_imag,
            prod_real * filt_imag + prod_imag * filt_real,
        ],
        0,
    )
    return transform(pair, total, 1.0, total // 2, 1)[0] * (1.0 / total)


def filter_grads(spectra, grad_chan):
    prod_real, prod_imag, filt_real, filt_imag = spectra
    length = grad_chan.shape[0]
    total = 2 * length
    spec = transform(grad_chan.astype(jnp.float32)[None], total, -1.0, total, 2)
    grad_real, grad_imag = (spec[0], spec[1])
    first_real = filt_real * grad_real + filt_imag * grad_imag
    first_imag = filt_real * grad_imag - filt_imag * grad_real
    second_real = prod_real * grad_real + prod_imag * grad_imag
    second_imag = prod_real * grad_imag - prod_imag * grad_real
    pair = jnp.stack([first_real - second_imag, first_imag + second_real], 0)
    result = transform(pair, total, 1.0, length, 2) * (1.0 / total)
    return (result[0], result[1])


def projection_grads(mixed_groups, out_grad, weight_slab):
    gathered = lax.all_gather(out_grad, "dp", axis=0, tiled=True)
    mix_grad_groups = lax.dot_general(
        gathered, weight_slab, (((1,), (1,)), ((), ())), preferred_element_type=jnp.float32
    ).astype(jnp.bfloat16)
    weight_term = lax.dot_general(
        mixed_groups, gathered, (((0,), (0,)), ((), ())), preferred_element_type=jnp.float32
    )
    return (mix_grad_groups, weight_term)


def body(streams, out_grad, proj_weight, long_filter, short_taps, doc_ids):
    row_count = streams.shape[1]
    span = short_taps.shape[0] - 1
    group_count = lax.axis_size("dp")
    shard_count = lax.axis_size("ctx")
    token_total = row_count * shard_count * group_count
    grad_scale = float(token_total) ** (-0.5)
    first_row = (lax.axis_index("dp") * shard_count + lax.axis_index("ctx")) * row_count
    edge_ids = jnp.full((span,), -1, jnp.int32)
    id_rows = lax.dynamic_slice_in_dim(
        jnp.concatenate([edge_ids, doc_ids, edge_ids]), first_row, row_count + 2 * span
    )
    own_ids = id_rows[span : span + row_count]
    earlier = from_behind(streams[:, row_count - span :, :], "ctx", 1)
    extended = jnp.concatenate([earlier, streams], axis=1).astype(jnp.float32)
    conv_out = jnp.zeros(streams.shape, jnp.float32)
    for offset in range(span + 1):
        same_doc = (id_rows[span - offset : span - offset + row_count] == own_ids).astype(
            jnp.float32
        )
        conv_out = (
            conv_out
            + short_taps[offset][:, None, :]
            * extended[:, span - offset : span - offset + row_count, :]
            * same_doc[None, :, None]
        )
    query = conv_out[0].astype(jnp.bfloat16)
    key_stream = conv_out[1]
    value_stream = conv_out[2]
    product = (key_stream * value_stream).astype(jnp.bfloat16)
    filter_full = lax.all_gather(long_filter, "dp", axis=0, tiled=True)
    product_chan = lax.all_to_all(product, "ctx", split_axis=1, concat_axis=0, tiled=True)
    spectra = forward_spectra(product_chan, filter_full)
    filtered_chan = apply_filter(spectra).astype(jnp.bfloat16)
    filtered = lax.all_to_all(filtered_chan, "ctx", split_axis=0, concat_axis=1, tiled=True)
    mixed = (query.astype(jnp.float32) * filtered.astype(jnp.float32)).astype(jnp.bfloat16)
    mixed_groups = lax.all_to_all(mixed, "dp", split_axis=1, concat_axis=0, tiled=True)
    mix_grad_groups, weight_term = projection_grads(mixed_groups, out_grad, proj_weight)
    mix_grad = lax.all_to_all(mix_grad_groups, "dp", split_axis=0, concat_axis=1, tiled=True)
    query_grad = (mix_grad.astype(jnp.float32) * filtered.astype(jnp.float32)).astype(jnp.bfloat16)
    filtered_grad = (mix_grad.astype(jnp.float32) * query.astype(jnp.float32)).astype(jnp.bfloat16)
    filtered_grad_chan = lax.all_to_all(
        filtered_grad, "ctx", split_axis=1, concat_axis=0, tiled=True
    )
    product_grad_chan, filter_term = filter_grads(spectra, filtered_grad_chan)
    product_grad = lax.all_to_all(
        product_grad_chan.astype(jnp.bfloat16), "ctx", split_axis=0, concat_axis=1, tiled=True
    )
    proj_grad = (
        lax.psum_scatter(
            weight_term.astype(jnp.bfloat16), "ctx", scatter_dimension=0, tiled=True
        ).astype(jnp.float32)
        * grad_scale
    )
    filter_grad = (
        lax.psum_scatter(
            filter_term.astype(jnp.bfloat16), "dp", scatter_dimension=0, tiled=True
        ).astype(jnp.float32)
        * grad_scale
    )
    conv_grad = jnp.stack(
        [
            query_grad.astype(jnp.float32),
            product_grad.astype(jnp.float32) * value_stream,
            product_grad.astype(jnp.float32) * key_stream,
        ]
    )
    later = from_behind(conv_grad[:, :span, :].astype(jnp.bfloat16), "ctx", -1).astype(jnp.float32)
    ahead_grads = jnp.concatenate([conv_grad, later], axis=1)
    stream_grad = jnp.zeros(streams.shape, jnp.float32)
    tap_terms = []
    for offset in range(span + 1):
        ahead_same = (id_rows[span + offset : span + offset + row_count] == own_ids).astype(
            jnp.float32
        )
        stream_grad = (
            stream_grad
            + short_taps[offset][:, None, :]
            * ahead_grads[:, offset : offset + row_count, :]
            * ahead_same[None, :, None]
        )
        behind_same = (id_rows[span - offset : span - offset + row_count] == own_ids).astype(
            jnp.float32
        )
        tap_terms.append(
            jnp.sum(
                conv_grad
                * extended[:, span - offset : span - offset + row_count, :]
                * behind_same[None, :, None],
                axis=1,
            )
        )
    tap_grad = lax.psum(jnp.stack(tap_terms), ("dp", "ctx")) * grad_scale
    return (stream_grad.astype(jnp.bfloat16), proj_grad, filter_grad, tap_grad)


def solution(mesh):
    placed = (
        P(None, ("dp", "ctx"), None),
        P(("dp", "ctx"), None),
        P("dp", None),
        P("dp", "ctx"),
        P(),
        P(),
    )
    return jax.shard_map(
        body,
        mesh=mesh,
        in_specs=placed,
        out_specs=(P(None, ("dp", "ctx"), None), P(("dp", "ctx"), None), P("dp", "ctx"), P()),
        check_vma=False,
    )
```

profile of v0, /device:TPU:1, one launch (start us, length us, event | category | flops | bytes accessed | tf_op | source)
XLA Modules:
  0.0 1012.1 jit_solution(6860253628012343804)
XLA Ops:
  8.9 4.6 collective-permute-start
  16.3 3.5 copy.135
  19.8 2.8 copy.134
  22.6 8.6 maximum_convert_fusion
  31.2 153.4 %all-gather.3.cloned.1.call-done = bf16[1024,4096]{1,0:T(8,128)(2,1)} async-done(((bf16[128,4096]{1,0:T(8,128)(2,1)}), bf16[1024,4096]{1,0:T(8,128)(2,1)}) %all-gather.3.cloned.1.call-update) | async-done | bytes 8388624 | tf_op jit(solution)/shard_map/all_gather | solution.py:100
  184.6 9.1 convolution_convert_fusion.1
  195.0 4.5 all-to-all-start
  199.6 13.6 %multiply_add_fusion = f32[3,128,4096]{1,2,0:T(8,128)S(1)} fusion(f32[3,130,4096]{1,2,0:T(8,128)} %maximum_convert_fusion, f32[128]{0:T(128)S(1)} %get-tuple-element.60, f32[3,4096]{1,0:T(4,128)S(1)} %get-tuple-element.45, f32[128]{0:T(128)S(1)} %get-tuple-element.62, f32[3,4096]{1,0:T(4,128)S(1)} %get-tuple-element.46, f32[3,4096]{1,0:T(4,128)S(1)} %get-tuple-element.44), kind=kLoop, calls=%fused_computation.37 | loop fusion | flops 11010048 | bytes 25314304 | tf_op jit(solution)/shard_map/add | solution.py:131
  217.4 10.6 %all-to-all-start.1 = ((bf16[128,32,128]{2,0,1:T(8,128)(2,1)}), bf16[128,32,128]{2,0,1:T(8,128)(2,1)S(1)}, u32[]{:S(2)}, u32[]{:S(2)}) async-start(bf16[128,32,128]{2,0,1:T(8,128)(2,1)} %copy.136), calls=%async_computation.1 | async-start | bytes 2097152 | tf_op jit(solution)/shard_map/all_to_all | solution.py:141
  234.0 18.9 %all-to-all-done.1 = bf16[128,32,128]{2,0,1:T(8,128)(2,1)S(1)} async-done(((bf16[128,32,128]{2,0,1:T(8,128)(2,1)}), bf16[128,32,128]{2,0,1:T(8,128)(2,1)S(1)}, u32[]{:S(2)}, u32[]{:S(2)}) %all-to-all-start.1) | async-done | bytes 1048608 | tf_op jit(solution)/shard_map/all_to_all | solution.py:141
  252.9 11.3 %all-to-all-start.3 = ((bf16[128,32,128]{2,0,1:T(8,128)(2,1)}), bf16[128,32,128]{2,0,1:T(8,128)(2,1)}, u32[]{:S(2)}, u32[]{:S(2)}) async-start(bf16[128,32,128]{2,0,1:T(8,128)(2,1)} %copy.155), calls=%async_computation.3 | async-start | bytes 2097152 | tf_op jit(solution)/shard_map/all_to_all | solution.py:151
  269.9 47.5 %all-gather.5.cloned.1.call-done = f32[4096,128]{1,0:T(8,128)} async-done(((f32[512,128]{1,0:T(8,128)}), f32[4096,128]{1,0:T(8,128)}) %all-gather.5.cloned.1.call-update) | async-done | bytes 2097168 | tf_op jit(solution)/shard_map/all_gather | solution.py:140
  317.4 2.8 copy.138
  320.2 5.7 fusion.34
  325.9 3.8 fusion.44
  329.7 6.5 multiply_subtract_fusion.1
  336.2 3.2 pad_maximum_fusion.1
  339.4 8.6 fusion.26
  349.1 2.6 copy.140
  364.2 8.8 fusion.29
  374.1 4.4 copy.158
  378.6 4.4 copy.160
  382.9 33.5 %slice.166 = f32[8191,128]{1,0:T(8,128)} reverse(f32[8191,128]{1,0:T(8,128)} %slice.197), dimensions={0} | reverse | bytes 8387584 | tf_op jit(solution)/shard_map/jit(_roll_static)/slice | solution.py:52
  416.5 33.5 %slice.170 = f32[8191,128]{1,0:T(8,128)} reverse(f32[8191,128]{1,0:T(8,128)} %slice.200), dimensions={0} | reverse | bytes 8387584 | tf_op jit(solution)/shard_map/jit(_roll_static)/slice | solution.py:52
  450.0 4.6 pad_maximum_fusion.6
  459.6 18.3 %multiply_subtract_fusion.3 = (f32[1,64,128,128]{3,1,0,2:T(8,128)}, f32[1,64,128,128]{3,1,0,2:T(8,128)S(1)}, f32[1,64,128,128]{3,1,0,2:T(8,128)S(1)}, f32[1,64,128,128]{3,1,0,2:T(8,128)}, f32[1,64,128,128]{3,1,0,2:T(8,128)}) fusion(f32[1,64,128,128]{3,2,1,0:T(8,128)} %bitcast.190, f32[1,64,128,128]{3,2,1,0:T(8,128)S(1)} %bitcast.181, ...), kind=kLoop, calls=%fused_computation.56 | loop fusion | flops 11534336 | bytes 37748736 | tf_op jit(solution)/shard_map/sub | solution.py:76
  477.8 13.3 %subtract_subtract_fusion = (f32[1,64,128,128]{3,1,0,2:T(8,128)S(1)}, f32[1,64,128,128]{3,1,0,2:T(8,128)}, f32[1,64,128,128]{3,1,0,2:T(8,128)}) fusion(f32[1,64,128,128]{3,1,0,2:T(8,128)} %get-tuple-element.23, f32[1,64,128,128]{3,1,0,2:T(8,128)} %get-tuple-element.22, f32[1,64,128,128]{3,1,0,2:T(8,128)S(1)} %get-tuple-element.21, ...), kind=kLoop, calls=%fused_computation.50 | loop fusion | flops 17825792 | bytes 37748736 | tf_op jit(solution)/shard_map/sub | solution.py:94
  491.2 6.7 fusion.32
  497.9 4.3 fusion.33
  502.3 6.5 multiply_subtract_fusion.2
  509.7 7.0 fusion.39
  518.3 9.3 all-to-all-start.2
  527.7 4.3 pad_maximum_fusion.4
  532.0 10.6 %fusion.25 = bf16[2,64,64,128]{3,1,2,0:T(8,128)(2,1)S(1)} fusion(f32[2,64,128,128]{3,1,2,0:T(8,128)S(1)} %pad_maximum_fusion.4, f32[1,64,2,128]{3,1,2,0:T(8,128)S(1)} %get-tuple-element.54, f32[1,64,2,128]{3,1,2,0:T(8,128)S(1)} %get-tuple-element.53), kind=kOutput, calls=%fused_computation.46 | convolution fusion | flops 1612742656 | bytes 10616832 | tf_op jit(solution)/shard_map/pkqn,qanc->pkac/dot_general | solution.py:47
  544.5 11.9 %all-to-all-done.2 = bf16[32,128,128]{2,1,0:T(8,128)(2,1)S(1)} async-done(((bf16[32,128,128]{2,1,0:T(8,128)(2,1)}), bf16[32,128,128]{2,1,0:T(8,128)(2,1)S(1)}, u32[]{:S(2)}, u32[]{:S(2)}) %all-to-all-start.2) | async-done | bytes 1048608 | tf_op jit(solution)/shard_map/all_to_all | solution.py:144
  556.4 5.5 all-to-all-start.4
  565.7 28.8 %all-to-all-done.4 = bf16[32,128,128]{2,1,0:T(8,128)(2,1)} async-done(((bf16[32,128,128]{2,1,0:T(8,128)(2,1)}), bf16[32,128,128]{2,1,0:T(8,128)(2,1)}, u32[]{:S(2)}, u32[]{:S(2)}) %all-to-all-start.4) | async-done | bytes 1048608 | tf_op jit(solution)/shard_map/all_to_all | solution.py:155
  597.8 3.4 bitcast_multiply_fusion.4
  604.5 3.2 copy.171
  609.6 3.4 fusion.38
  613.0 3.6 all-to-all-start.5
  616.7 3.8 copy.172
  620.5 10.7 %pad_maximum_fusion = f32[3,130,4096]{1,2,0:T(8,128)} fusion(f32[3,2,4096]{1,2,0:T(8,128)} %copy.172, f32[1,128,4096]{1,2,0:T(8,128)} %copy-done.6, f32[1,128,4096]{1,2,0:T(8,128)S(1)} %get-tuple-element.35, f32[1,128,4096]{1,2,0:T(8,128)} %copy-done.8), kind=kLoop, calls=%fused_computation | loop fusion | flops 4792320 | bytes 12779520 | tf_op jit(solution)/shard_map/concatenate | solution.py:178
  631.3 24.9 %multiply_reduce_fusion.2 = (f32[3,4096]{1,0:T(4,128)S(1)}, f32[3,4096]{1,0:T(4,128)S(1)}, f32[3,4096]{1,0:T(4,128)S(1)}, bf16[3,128,4096]{1,2,0:T(8,128)(2,1)}) fusion(f32[3,130,4096]{1,2,0:T(8,128)} %maximum_convert_fusion, f32[1,128,4096]{1,2,0:T(8,128)S(1)} %copy-done.7, f32[1,128,4096]{1,2,0:T(8,128)S(1)} %get-tuple-element.35, ...), kind=kLoop, calls=%fused_computation.36 | loop fusion | flops 28274688 | bytes 41191424 | tf_op jit(solution)/shard_map/reduce_sum | solution.py:195
  657.6 9.5 convolution_convert_fusion
  669.0 2.8 copy.176
  673.4 229.5 %all-reduce.2.cloned.1.call-done = f32[3,3,4096]{2,1,0:T(4,128)} async-done(((f32[3,3,4096]{2,1,0:T(4,128)}), f32[3,3,4096]{2,1,0:T(4,128)}) %all-reduce.2.cloned.1.call-update) | async-done | bytes 147472 | tf_op jit(solution)/shard_map/psum | solution.py:202
  904.5 98.9 %reduce-scatter.3.cloned.1.call-done = bf16[16,4096]{1,0:T(8,128)(2,1)} async-done(((bf16[512,4096]{1,0:T(8,128)(2,1)}), bf16[16,4096]{1,0:T(8,128)(2,1)}) %reduce-scatter.3.cloned.1.call-update) | async-done | bytes 131088 | tf_op jit(solution)/shard_map/reduce_scatter | solution.py:159
  (148 shorter events, 66.1 us)
Async XLA Ops:
  7.2 177.4 %all-gather.3.cloned.1.call-start = ((), (), s32[]{:S(2)}) async-start(), calls=%async_computation.8 | async-start | bytes 9437184 | tf_op jit(solution)/shard_map/all_gather | solution.py:100
  8.9 10.9 %collective-permute-start = (bf16[3,2,4096]{2,1,0:T(2,128)(2,1)S(1)}, bf16[3,2,4096]{2,1,0:T(2,128)(2,1)S(1)}, u32[]{:S(2)}, u32[]{:S(2)}) collective-permute-start(bf16[3,2,4096]{2,1,0:T(2,128)(2,1)S(1)} %slice.150), channel_id=1, source_target_pairs={{0,1},{1,2},{2,3},{3,4},{4,5},{5,6},{6,7},{7,8},{8,9},{9,10},{10,1... | collective-permute-start | bytes 147464 | tf_op jit(solution)/shard_map/ppermute | solution.py:12
  15.6 183.9 %copy-start.20 = (f32[3,4096]{1,0:T(4,128)}, f32[3,4096]{1,0:T(4,128)S(1)}, u32[]{:S(2)}) copy-start(f32[3,4096]{1,0:T(4,128)S(1)} %get-tuple-element.44) | copy-start | bytes 147460
  15.6 183.9 %copy-start.22 = (f32[3,4096]{1,0:T(4,128)}, f32[3,4096]{1,0:T(4,128)S(1)}, u32[]{:S(2)}) copy-start(f32[3,4096]{1,0:T(4,128)S(1)} %get-tuple-element.45) | copy-start | bytes 147460
  15.6 183.9 %copy-start.24 = (f32[3,4096]{1,0:T(4,128)}, f32[3,4096]{1,0:T(4,128)S(1)}, u32[]{:S(2)}) copy-start(f32[3,4096]{1,0:T(4,128)S(1)} %get-tuple-element.46) | copy-start | bytes 147460
  16.2 183.3 %copy-start.33 = (f32[128]{0:T(128)}, f32[128]{0:T(128)S(1)}, u32[]{:S(2)}) copy-start(f32[128]{0:T(128)S(1)} %get-tuple-element.60) | copy-start | bytes 1540
  16.3 183.3 %copy-start.35 = (f32[128]{0:T(128)}, f32[128]{0:T(128)S(1)}, u32[]{:S(2)}) copy-start(f32[128]{0:T(128)S(1)} %get-tuple-element.62) | copy-start | bytes 1540
  195.0 22.4 %all-to-all-start = ((bf16[8,128,512]{1,2,0:T(8,128)(2,1)}), bf16[8,128,512]{1,2,0:T(8,128)(2,1)S(1)}, u32[]{:S(2)}, u32[]{:S(2)}) async-start(bf16[8,128,512]{1,2,0:T(8,128)(2,1)} %copy.133), calls=%async_computation | async-start | bytes 2097152 | tf_op jit(solution)/shard_map/all_to_all | solution.py:148
  213.2 2.6 copy-start
  217.4 35.6 %all-to-all-start.1 = ((bf16[128,32,128]{2,0,1:T(8,128)(2,1)}), bf16[128,32,128]{2,0,1:T(8,128)(2,1)S(1)}, u32[]{:S(2)}, u32[]{:S(2)}) async-start(bf16[128,32,128]{2,0,1:T(8,128)(2,1)} %copy.136), calls=%async_computation.1 | async-start | bytes 2097152 | tf_op jit(solution)/shard_map/all_to_all | solution.py:141
  227.9 89.4 %all-gather.5.cloned.1.call-start = ((), (), s32[]{:S(2)}) async-start(), calls=%async_computation.9 | async-start | bytes 2359296 | tf_op jit(solution)/shard_map/all_gather | solution.py:140
  252.9 73.0 %all-to-all-start.3 = ((bf16[128,32,128]{2,0,1:T(8,128)(2,1)}), bf16[128,32,128]{2,0,1:T(8,128)(2,1)}, u32[]{:S(2)}, u32[]{:S(2)}) async-start(bf16[128,32,128]{2,0,1:T(8,128)(2,1)} %copy.155), calls=%async_computation.3 | async-start | bytes 2097152 | tf_op jit(solution)/shard_map/all_to_all | solution.py:151
  269.9 50.3 %copy-start.26 = (f32[1,64,2,32]{1,3,2,0:T(8,128)S(1)}, f32[1,64,2,32]{1,3,2,0:T(8,128)}, u32[]{:S(2)}) copy-start(f32[1,64,2,32]{1,3,2,0:T(8,128)} %get-tuple-element.57) | copy-start | bytes 49156
  269.9 50.3 %copy-start.27 = (f32[1,64,2,32]{1,3,2,0:T(8,128)S(1)}, f32[1,64,2,32]{1,3,2,0:T(8,128)}, u32[]{:S(2)}) copy-start(f32[1,64,2,32]{1,3,2,0:T(8,128)} %get-tuple-element.58) | copy-start | bytes 49156
  325.9 3.8 copy-start.19
  325.9 3.8 copy-start.31
  325.9 3.8 copy-start.5
  351.7 3.3 copy-start.1
  357.4 4.1 copy-start.3
  357.4 5.1 copy-start.17
  450.0 4.6 copy-start.16
  454.6 3.7 copy-start.2
  454.6 5.0 copy-start.4
  491.2 6.7 copy-start.14
  491.2 6.7 copy-start.15
  497.9 4.3 copy-start.30
  516.7 11.0 %copy-start.32 = (f32[64,1,128]{2,0,1:T(8,128)S(1)}, f32[64,1,128]{2,0,1:T(8,128)}, u32[]{:S(2)}) copy-start(f32[64,1,128]{2,0,1:T(8,128)} %get-tuple-element.71) | copy-start | bytes 98308
  518.3 38.1 %all-to-all-start.2 = ((bf16[32,128,128]{2,1,0:T(8,128)(2,1)}), bf16[32,128,128]{2,1,0:T(8,128)(2,1)S(1)}, u32[]{:S(2)}, u32[]{:S(2)}) async-start(bf16[32,128,128]{2,1,0:T(8,128)(2,1)} %bitcast.44), calls=%async_computation.2 | async-start | bytes 2097152 | tf_op jit(solution)/shard_map/all_to_all | solution.py:144
  556.4 38.0 %all-to-all-start.4 = ((bf16[32,128,128]{2,1,0:T(8,128)(2,1)}), bf16[32,128,128]{2,1,0:T(8,128)(2,1)}, u32[]{:S(2)}, u32[]{:S(2)}) async-start(bf16[32,128,128]{2,1,0:T(8,128)(2,1)} %bitcast.71), calls=%async_computation.4 | async-start | bytes 2097152 | tf_op jit(solution)/shard_map/all_to_all | solution.py:155
  561.9 109.8 %reduce-scatter.5.cloned.1.call-start = ((), (), s32[]{:S(2)}) async-start(), calls=%async_computation.11 | async-start | bytes 1179648 | tf_op jit(solution)/shard_map/reduce_scatter | solution.py:165
  597.8 3.5 copy-start.11
  597.8 4.1 copy-start.12
  601.1 3.4 copy-start.6
  602.1 2.4 copy-start.8
  607.7 8.9 collective-permute-start.1
  613.0 44.0 %all-to-all-start.5 = ((bf16[128,8,512]{0,2,1:T(8,128)(2,1)}), bf16[128,8,512]{0,2,1:T(8,128)(2,1)S(1)}, u32[]{:S(2)}, u32[]{:S(2)}) async-start(bf16[128,8,512]{0,2,1:T(8,128)(2,1)} %fusion.38), calls=%async_computation.5 | async-start | bytes 2097152 | tf_op jit(solution)/shard_map/all_to_all | solution.py:146
  616.6 286.3 %all-reduce.2.cloned.1.call-start = ((), (), s32[]{:S(2)}) async-start(), calls=%async_computation.12 | async-start | bytes 393216 | tf_op jit(solution)/shard_map/psum | solution.py:202
  620.5 10.7 %copy-start.7 = (f32[1,128,4096]{1,2,0:T(8,128)S(1)}, f32[1,128,4096]{1,2,0:T(8,128)}, u32[]{:S(2)}) copy-start(f32[1,128,4096]{1,2,0:T(8,128)} %copy-done.6) | copy-start | bytes 6291460
  620.5 10.7 %copy-start.9 = (f32[1,128,4096]{1,2,0:T(8,128)S(1)}, f32[1,128,4096]{1,2,0:T(8,128)}, u32[]{:S(2)}) copy-start(f32[1,128,4096]{1,2,0:T(8,128)} %copy-done.8) | copy-start | bytes 6291460
  620.5 10.7 %copy-start.21 = (f32[3,4096]{1,0:T(4,128)S(1)}, f32[3,4096]{1,0:T(4,128)}, u32[]{:S(2)}) copy-start(f32[3,4096]{1,0:T(4,128)} %copy-done.20) | copy-start | bytes 147460
  620.5 10.7 %copy-start.23 = (f32[3,4096]{1,0:T(4,128)S(1)}, f32[3,4096]{1,0:T(4,128)}, u32[]{:S(2)}) copy-start(f32[3,4096]{1,0:T(4,128)} %copy-done.22) | copy-start | bytes 147460
  620.5 10.7 %copy-start.25 = (f32[3,4096]{1,0:T(4,128)S(1)}, f32[3,4096]{1,0:T(4,128)}, u32[]{:S(2)}) copy-start(f32[3,4096]{1,0:T(4,128)} %copy-done.24) | copy-start | bytes 147460
  620.5 10.7 %copy-start.34 = (f32[128]{0:T(128)S(1)}, f32[128]{0:T(128)}, u32[]{:S(2)}) copy-start(f32[128]{0:T(128)} %copy-done.33) | copy-start | bytes 1540
  620.5 10.7 %copy-start.36 = (f32[128]{0:T(128)S(1)}, f32[128]{0:T(128)}, u32[]{:S(2)}) copy-start(f32[128]{0:T(128)} %copy-done.35) | copy-start | bytes 1540
  620.5 10.7 %copy-start.37 = (f32[128]{0:T(128)S(1)}, f32[128]{0:T(128)}, u32[]{:S(2)}) copy-start(f32[128]{0:T(128)} %get-tuple-element.59) | copy-start | bytes 1540
  620.5 10.7 %copy-start.38 = (f32[128]{0:T(128)S(1)}, f32[128]{0:T(128)}, u32[]{:S(2)}) copy-start(f32[128]{0:T(128)} %get-tuple-element.61) | copy-start | bytes 1540
  657.0 346.5 %reduce-scatter.3.cloned.1.call-start = ((), (), s32[]{:S(2)}) async-start(), calls=%async_computation.10 | async-start | bytes 4325376 | tf_op jit(solution)/shard_map/reduce_scatter | solution.py:159
  667.1 1.9 copy-start.18
  (4 other events, 4.9 us)
Sparse Core Ops, SparseCore 0:
  9.8 174.7 all-gather.2
  230.6 86.7 all-gather.4
  565.3 45.0 reduce-scatter.4
  657.1 245.7 all-reduce.1
  906.7 96.7 reduce-scatter.2
where the time goes:
time: 1030 us; the launch traced here: 1010 us
  waiting for transfers between devices  590 us (57%)
  other arithmetic  145 us (14%)
  local copies, waits for them, and re-layouts  136 us (13%)
  matrix products  74.1 us (7%)
  starting transfers between devices  51.5 us (5%)
  between operations  15 us (1%)
    psum x1, waiting for transfers between devices, body(): tap_grad = lax.psum(jnp.stack(tap_terms), ('dp', 'ctx')) * grad_scale  230 us
    all_gather x1, waiting for transfers between devices, projection_grads(): gathered = lax.all_gather(out_grad, 'dp', axis=0, tiled=True)  153 us
    reduce_scatter x1, waiting for transfers between devices, body(): lax.psum_scatter(weight_term.astype(jnp.bfloat16), 'ctx', scatter_dimensi...  98.9 us
    slice x4, local copies, waits for them, and re-layouts, mirror_index(): return jnp.roll(jnp.flip(values, 0), 1, 0)  71.7 us
    all_gather x1, waiting for transfers between devices, body(): filter_full = lax.all_gather(long_filter, 'dp', axis=0, tiled=True)  47.5 us
    dot_general x4, matrix products, transform(): jnp.einsum('pkqn,qanc->pkac', second_table, turned, precision=level)  35 us
    all_to_all x1, waiting for transfers between devices, body(): lax.all_to_all(product_grad_chan.astype(jnp.bfloat16), 'ctx', split_axis=...  28.8 us
    reduce_sum x1, other arithmetic, body(): jnp.sum(conv_grad * extended[:, span - offset:span - offset + row_count,...  24.9 us
  transfers between devices with their start and end apart: 13, of which 7 were waited for; matrix products, arithmetic and copies ran while one was open for 14% of the time, Pallas kernels for 0%

commit v1 on v0

v1 whole, which is shorter than its diff:
```python
import functools
import math

import jax
import jax.numpy as jnp
import numpy as np
from jax import lax
from jax.experimental import pallas as pl
from jax.experimental.pallas import tpu as pltpu
from jax.sharding import Mesh
from jax.sharding import PartitionSpec as P

DP = ("x", "w")
CTX = ("z", "y", "c")
F32 = jnp.float32
BF16 = jnp.bfloat16
LENGTH = 4096
TOTAL = 2 * LENGTH
SLOTS = 32
STEP = 128
WIDE = 512
GRAD_SCALE = float(32768) ** (-0.5)
MESH = pl.DeviceIdType.MESH


def split_table(table):
    return table.astype(BF16)


def make_tables():
    a = np.arange(32)
    b = np.arange(STEP)
    first = np.zeros((2 * SLOTS, 32))
    first[0] = 1.0
    first[1] = (-1.0) ** a
    for s in range(1, SLOTS):
        first[2 * s] = np.cos(2 * np.pi * a * s / 64)
        first[2 * s + 1] = -np.sin(2 * np.pi * a * s / 64)
    first_wide = np.kron(first, np.eye(8))
    last_wide = np.kron(first.T * (2.0 / TOTAL), np.eye(8))
    angle = 2 * np.pi * np.outer(b, b) / STEP
    cosine, sine = np.cos(angle), np.sin(angle)
    plain = np.block([[cosine, sine], [-sine, cosine]])
    special = np.zeros((2 * STEP, 2 * STEP))
    half = np.arange(64)
    even = 2 * np.pi * np.outer(half, b) / STEP
    odd = 2 * np.pi * np.outer(32 + 64 * half, b) / TOTAL
    special[:64, :STEP] = np.cos(even)
    special[64:128, STEP:] = np.cos(odd)
    special[128:192, :STEP] = -np.sin(even)
    special[128, :STEP] = (-1.0) ** b
    special[192:, STEP:] = -np.sin(odd)
    middle = np.stack([split_table(special), split_table(plain)])
    middle_back = np.stack([split_table(special.T), split_table(plain.T)])
    turn = 2 * np.pi * np.outer(np.arange(SLOTS), b) / TOTAL
    twist = np.concatenate([np.cos(turn), np.sin(turn)], 1).astype(np.float32)
    return split_table(first_wide), split_table(last_wide), middle, middle_back, twist


def dot32(a, b):
    return jnp.dot(a, b, preferred_element_type=F32)


def dot16(table, value):
    return dot32(table, value.astype(BF16))


def twisted(re, im, c, s):
    return re * c + im * s, im * c - re * s


def untwisted(re, im, c, s):
    return re * c - im * s, im * c + re * s


def halves_of(block):
    return [block[:, :8, :].reshape(256, STEP), block[:, 8:, :].reshape(256, STEP)]


def edge_rows(k):
    rows = lax.broadcasted_iota(jnp.int32, (STEP, STEP), 0)
    return jnp.logical_and(rows == 0, k == 0)


def filter_forward_kernel(
    prod_ref, filt_ref, first_ref, last_ref, mid_ref, back_ref, twist_ref,
    out_ref, spec_prod_ref, spec_filt_ref, yp_ref, yf_ref,
):
    first = first_ref[...]

    @pl.loop(0, 8, unroll=2)
    def _(h):
        rows = pl.ds(pl.multiple_of(16 * h, 16), 16)
        prods = halves_of(prod_ref[:, rows, :].astype(F32))
        filts = halves_of(filt_ref[:, rows, :].astype(F32))
        for j in range(2):
            wide = dot32(first, jnp.concatenate([prods[j], filts[j]], 1).astype(BF16))
            at = pl.ds(pl.multiple_of(16 * h + 8 * j, 8), 8)
            yp_ref[:, at, :] = wide[:, :128].reshape(64, 8, STEP)
            yf_ref[:, at, :] = wide[:, 128:].reshape(64, 8, STEP)

    @pl.loop(0, SLOTS, unroll=4)
    def _(k):
        c, s = twist_ref[k, :STEP, :], twist_ref[k, STEP:, :]
        which = jnp.minimum(k, 1)
        pair = pl.ds(2 * k, 2)
        yp, yf = yp_ref[pair], yf_ref[pair]
        pr, pi = twisted(yp[0], yp[1], c, s)
        fr, fi = twisted(yf[0], yf[1], c, s)
        value = jnp.concatenate([jnp.concatenate([pr, pi], 0), jnp.concatenate([fr, fi], 0)], 1)
        spec = dot16(mid_ref[which], value)
        spec_prod_ref[k] = spec[:, :128]
        spec_filt_ref[k] = spec[:, 128:]
        pr, pi = spec[:128, :128], spec[128:, :128]
        fr, fi = spec[:128, 128:], spec[128:, 128:]
        edge = edge_rows(k)
        re = jnp.where(edge, 0.5 * (pr * fr), pr * fr - pi * fi)
        im = jnp.where(edge, 0.5 * (pi * fi), pr * fi + pi * fr)
        back = dot16(back_ref[which], jnp.concatenate([re, im], 0))
        re, im = untwisted(back[:128], back[128:], c, s)
        yp_ref[2 * k] = re
        yp_ref[2 * k + 1] = im

    last = last_ref[...]

    @pl.loop(0, 8, unroll=2)
    def _(h):
        halves = [yp_ref[:, pl.ds(pl.multiple_of(16 * h + 8 * j, 8), 8), :].reshape(512, STEP) for j in range(2)]
        out = dot16(last, jnp.concatenate(halves, 1))
        parts = [out[:, 128 * j : 128 * (j + 1)].reshape(32, 8, STEP) for j in range(2)]
        rows = pl.ds(pl.multiple_of(16 * h, 16), 16)
        out_ref[:, rows, :] = jnp.concatenate(parts, 1).astype(BF16)


def filter_backward_kernel(
    grad_ref, spec_prod_ref, spec_filt_ref, first_ref, last_ref, mid_ref, back_ref, twist_ref,
    prod_grad_ref, filt_grad_ref, yg_ref, yv_ref,
):
    first = first_ref[...]

    @pl.loop(0, 8, unroll=2)
    def _(h):
        rows = pl.ds(pl.multiple_of(16 * h, 16), 16)
        grads = halves_of(grad_ref[:, rows, :].astype(F32))
        grad = jnp.concatenate([grads[0], grads[1]], 1).astype(BF16)
        out = dot32(first, grad)
        for j in range(2):
            at = pl.ds(pl.multiple_of(16 * h + 8 * j, 8), 8)
            yg_ref[:, at, :] = out[:, 128 * j : 128 * (j + 1)].reshape(64, 8, STEP)

    @pl.loop(0, SLOTS, unroll=4)
    def _(k):
        c, s = twist_ref[k, :STEP, :], twist_ref[k, STEP:, :]
        which = jnp.minimum(k, 1)
        yg = yg_ref[pl.ds(2 * k, 2)]
        gr, gi = twisted(yg[0], yg[1], c, s)
        spec = dot16(mid_ref[which], jnp.concatenate([gr, gi], 0))
        gr, gi = spec[:128], spec[128:]
        edge = edge_rows(k)
        cols = []
        for ref in (spec_filt_ref, spec_prod_ref):
            hr, hi = ref[k, :STEP, :], ref[k, STEP:, :]
            re = jnp.where(edge, 0.5 * (hr * gr), hr * gr + hi * gi)
            im = jnp.where(edge, 0.5 * (hi * gi), hr * gi - hi * gr)
            cols.append(jnp.concatenate([re, im], 0))
        back = dot16(back_ref[which], jnp.concatenate(cols, 1))
        re, im = untwisted(back[:128, :128], back[128:, :128], c, s)
        yg_ref[2 * k] = re
        yg_ref[2 * k + 1] = im
        re, im = untwisted(back[:128, 128:], back[128:, 128:], c, s)
        yv_ref[2 * k] = re
        yv_ref[2 * k + 1] = im

    last = last_ref[...]

    @pl.loop(0, 8, unroll=2)
    def _(h):
        parts, other = [], []
        for j in range(2):
            at = pl.ds(pl.multiple_of(16 * h + 8 * j, 8), 8)
            value = jnp.concatenate([yg_ref[:, at, :].reshape(512, STEP), yv_ref[:, at, :].reshape(512, STEP)], 1)
            out = dot16(last, value)
            parts.append(out[:, :128].reshape(32, 8, STEP))
            other.append(out[:, 128:].reshape(32, 8, STEP))
        rows = pl.ds(pl.multiple_of(16 * h, 16), 16)
        prod_grad_ref[:, rows, :] = jnp.concatenate(parts, 1).astype(BF16)
        filt_grad_ref[:, rows, :] = jnp.concatenate(other, 1).astype(BF16)


def vmem():
    return pl.BlockSpec(memory_space=pltpu.VMEM)


def tables_in():
    first, last, middle, back, twist = make_tables()
    wide = jnp.broadcast_to(jnp.asarray(twist)[:, :, None], (SLOTS, 2 * STEP, STEP))
    return [jnp.asarray(first), jnp.asarray(last), jnp.asarray(middle), jnp.asarray(back), wide]


def filter_forward(prod, filt, tables):
    spec = jax.ShapeDtypeStruct((SLOTS, 2 * STEP, STEP), F32)
    return pl.pallas_call(
        filter_forward_kernel,
        out_shape=[jax.ShapeDtypeStruct((32, STEP, STEP), BF16), spec, spec],
        in_specs=[vmem()] * 7,
        out_specs=[vmem()] * 3,
        scratch_shapes=[pltpu.VMEM((64, STEP, STEP), F32)] * 2,
        compiler_params=pltpu.CompilerParams(vmem_limit_bytes=40 * 1024 * 1024),
        cost_estimate=pl.CostEstimate(flops=12 * 10**9, bytes_accessed=18 * 2**20, transcendentals=0),
        name="filter_forward",
    )(prod, filt, *tables)


def filter_backward(grad, spec_prod, spec_filt, tables):
    out = jax.ShapeDtypeStruct((32, STEP, STEP), BF16)
    return pl.pallas_call(
        filter_backward_kernel,
        out_shape=[out, out],
        in_specs=[vmem()] * 8,
        out_specs=[vmem()] * 2,
        scratch_shapes=[pltpu.VMEM((64, STEP, STEP), F32)] * 2,
        compiler_params=pltpu.CompilerParams(vmem_limit_bytes=40 * 1024 * 1024),
        cost_estimate=pl.CostEstimate(flops=12 * 10**9, bytes_accessed=18 * 2**20, transcendentals=0),
        name="filter_backward",
    )(grad, spec_prod, spec_filt, *tables)


def convolved(ext_ref, taps_ref, masks, stream):
    total = taps_ref[0, stream : stream + 1, :] * ext_ref[stream, pl.ds(8, STEP), :]
    for i in (1, 2):
        total = total + taps_ref[i, stream : stream + 1, :] * ext_ref[stream, pl.ds(8 - i, STEP), :] * masks[i - 1]
    return total


def fill_extended(streams_ref, early_ref, ext_ref):
    for s in range(3):
        ext_ref[s, pl.ds(6, 2), :] = early_ref[s].astype(F32)
        ext_ref[s, pl.ds(8, STEP), :] = streams_ref[s].astype(F32)


def short_kernel(streams_ref, early_ref, taps_ref, masks_ref, query_ref, prod_ref, head_ref, ext_ref):
    fill_extended(streams_ref, early_ref, ext_ref)
    masks = [masks_ref[:, i : i + 1] for i in range(2)]
    query_ref[...] = convolved(ext_ref, taps_ref, masks, 0).astype(BF16)
    key = convolved(ext_ref, taps_ref, masks, 1)
    value = convolved(ext_ref, taps_ref, masks, 2)
    head_ref[0] = key[:8]
    head_ref[1] = value[:8]
    prod = (key * value).astype(BF16)
    for j in range(4):
        prod_ref[j] = prod[:, 128 * j : 128 * (j + 1)]


def rows_spec(lead, rows):
    return pl.BlockSpec((lead, rows, WIDE), lambda i: (0, 0, i))


def flat_spec(rows):
    return pl.BlockSpec((rows, WIDE), lambda i: (0, i))


def chan_spec(rows=STEP):
    return pl.BlockSpec((4, rows, STEP), lambda i: (i, 0, 0))


def slab_spec(rows=STEP):
    return pl.BlockSpec((1, rows, WIDE), lambda i: (i, 0, 0))


def pair_spec(rows=STEP):
    return pl.BlockSpec((1, rows, WIDE), lambda i: (i // 2, 0, i % 2))


def mask_spec():
    return pl.BlockSpec((STEP, 8), lambda i: (0, 0))


def short_filter(streams, early, taps, masks):
    return pl.pallas_call(
        short_kernel,
        grid=(8,),
        out_shape=[
            jax.ShapeDtypeStruct((STEP, 4096), BF16),
            jax.ShapeDtypeStruct((32, STEP, STEP), BF16),
            jax.ShapeDtypeStruct((2, 8, 4096), F32),
        ],
        in_specs=[rows_spec(3, STEP), rows_spec(3, 2), rows_spec(3, 3), mask_spec()],
        out_specs=[flat_spec(STEP), chan_spec(), rows_spec(2, 8)],
        scratch_shapes=[pltpu.VMEM((3, STEP + 8, WIDE), F32)],
        cost_estimate=pl.CostEstimate(flops=10**7, bytes_accessed=5 * 2**20, transcendentals=0),
        name="short_filter",
    )(streams, early, taps, masks)


def mixed_kernel(query_ref, filtered_ref, out_ref):
    filtered = jnp.concatenate([filtered_ref[j] for j in range(4)], 1)
    out_ref[0] = (query_ref[...].astype(F32) * filtered.astype(F32)).astype(BF16)


def mixed_of(query, filtered):
    return pl.pallas_call(
        mixed_kernel,
        grid=(8,),
        out_shape=jax.ShapeDtypeStruct((8, STEP, WIDE), BF16),
        in_specs=[flat_spec(STEP), chan_spec()],
        out_specs=slab_spec(),
        cost_estimate=pl.CostEstimate(flops=10**6, bytes_accessed=3 * 2**20, transcendentals=0),
        name="mixed",
    )(query, filtered)


def filtered_grad_kernel(mix_grad_ref, query_ref, out_ref):
    out = (mix_grad_ref[0].astype(F32) * query_ref[...].astype(F32)).astype(BF16)
    for j in range(4):
        out_ref[j] = out[:, 128 * j : 128 * (j + 1)]


def filtered_grad_of(mix_grad, query):
    return pl.pallas_call(
        filtered_grad_kernel,
        grid=(8,),
        out_shape=jax.ShapeDtypeStruct((32, STEP, STEP), BF16),
        in_specs=[pair_spec(), flat_spec(STEP)],
        out_specs=chan_spec(),
        cost_estimate=pl.CostEstimate(flops=10**6, bytes_accessed=3 * 2**20, transcendentals=0),
        name="filtered_grad",
    )(mix_grad, query)


def lanes_of(ref):
    return jnp.concatenate([ref[j] for j in range(4)], 1)


def final_kernel(
    streams_ref, early_ref, taps_ref, masks_ref, mix_grad_ref, filtered_ref, prod_grad_ref,
    mix_next_ref, filtered_next_ref, prod_next_ref, head_next_ref,
    grads_ref, tap_ref, ext_ref, conv_ref,
):
    fill_extended(streams_ref, early_ref, ext_ref)
    behind = [masks_ref[:, i : i + 1] for i in range(2)]
    ahead = [masks_ref[:, 2 + i : 3 + i] for i in range(2)]
    key = convolved(ext_ref, taps_ref, behind, 1)
    value = convolved(ext_ref, taps_ref, behind, 2)
    prod_grad = lanes_of(prod_grad_ref).astype(F32)
    prod_next = lanes_of(prod_next_ref).astype(F32)[:2]
    body = pl.ds(0, STEP)
    tail = pl.ds(STEP, 2)
    query_grad = mix_grad_ref[0].astype(F32) * lanes_of(filtered_ref).astype(F32)
    conv_ref[0, body, :] = query_grad.astype(BF16).astype(F32)
    query_next = mix_next_ref[0].astype(F32) * lanes_of(filtered_next_ref).astype(F32)
    conv_ref[0, tail, :] = query_next.astype(BF16).astype(F32)[:2]
    conv_ref[1, body, :] = prod_grad * value
    conv_ref[1, tail, :] = prod_next * head_next_ref[1, :2, :]
    conv_ref[2, body, :] = prod_grad * key
    conv_ref[2, tail, :] = prod_next * head_next_ref[0, :2, :]
    for s in range(3):
        here = conv_ref[s, body, :]
        grad = taps_ref[0, s : s + 1, :] * here
        sums = [jnp.sum(here * ext_ref[s, pl.ds(8, STEP), :], axis=0, keepdims=True)]
        for i in (1, 2):
            grad = grad + taps_ref[i, s : s + 1, :] * conv_ref[s, pl.ds(i, STEP), :] * ahead[i - 1]
            behind_rows = ext_ref[s, pl.ds(8 - i, STEP), :] * behind[i - 1]
            sums.append(jnp.sum(here * behind_rows, axis=0, keepdims=True))
        grads_ref[s] = grad.astype(BF16)
        for i in range(3):
            for j in range(4):
                tap_ref[j, 3 * i + s : 3 * i + s + 1, :] = sums[i][:, 128 * j : 128 * (j + 1)]
    for j in range(4):
        tap_ref[j, 9:16, :] = jnp.zeros((7, STEP), F32)


def final_grads(streams, early, taps, masks, mix_grad, filtered, prod_grad, nexts):
    return pl.pallas_call(
        final_kernel,
        grid=(8,),
        out_shape=[
            jax.ShapeDtypeStruct((3, STEP, 4096), BF16),
            jax.ShapeDtypeStruct((32, 16, STEP), F32),
        ],
        in_specs=[
            rows_spec(3, STEP), rows_spec(3, 2), rows_spec(3, 3), mask_spec(),
            pair_spec(), chan_spec(), chan_spec(), pair_spec(16), chan_spec(16), chan_spec(16), rows_spec(2, 8),
        ],
        out_specs=[rows_spec(3, STEP), chan_spec(16)],
        scratch_shapes=[pltpu.VMEM((3, STEP + 8, WIDE), F32)] * 2,
        cost_estimate=pl.CostEstimate(flops=3 * 10**7, bytes_accessed=9 * 2**20, transcendentals=0),
        name="final_grads",
    )(streams, early, taps, masks, mix_grad, filtered, prod_grad, *nexts)


def step_along(value, axis, by):
    peers = lax.axis_size(axis)
    return lax.ppermute(value, axis, [(i, i + by) for i in range(peers) if 0 <= i + by < peers])


class Here:
    def __init__(self):
        self.x, self.w, self.z, self.y, self.c = [lax.axis_index(name) for name in DP + CTX]
        self.ctx = self.z * 8 + self.y * 2 + self.c
        self.dp = self.x * 2 + self.w

    def at_ctx(self, i):
        return (self.x, self.w, i // 8, lax.rem(i // 2, 4), lax.rem(i, 2))

    def at_dp(self, i):
        return (i // 2, lax.rem(i, 2), self.z, self.y, self.c)

    def along_x(self, by):
        return (lax.rem(self.x + by, 4), self.w, self.z, self.y, self.c)

    def along_y(self, by):
        return (self.x, self.w, self.z, lax.rem(self.y + by, 4), self.c)

    def along_z(self, by):
        return (self.x, self.w, lax.rem(self.z + by, 4), self.y, self.c)

    def across_w(self):
        return (self.x, 1 - self.w, self.z, self.y, self.c)

    def across_c(self):
        return (self.x, self.w, self.z, self.y, 1 - self.c)

    def before(self):
        return self.at_ctx(lax.rem(self.ctx + 31, 32))

    def meet(self):
        barrier = pltpu.get_barrier_semaphore()

        @pl.loop(1, 32)
        def _(p):
            place = self.at_ctx(lax.rem(self.ctx + p, 32))
            pl.semaphore_signal(barrier, inc=1, device_id=place, device_id_type=MESH)

        @pl.loop(1, 8)
        def _(p):
            place = self.at_dp(lax.rem(self.dp + p, 8))
            pl.semaphore_signal(barrier, inc=1, device_id=place, device_id_type=MESH)

        pl.semaphore_wait(barrier, 38)


class Links:
    def __init__(self, send, recv, local):
        self.send, self.recv, self.local = send, recv, local

    def to(self, n, place, src, dst):
        return pltpu.make_async_remote_copy(
            src_ref=src, dst_ref=dst, send_sem=self.send.at[n], recv_sem=self.recv.at[n],
            device_id=place, device_id_type=MESH,
        )

    def own(self, n, src, dst):
        return pltpu.make_async_copy(src, dst, self.local.at[n])

    def pairs(self, base, count, me, place, src, dst, same=False):
        def copy(p):
            peer = lax.rem(me + p, count)
            return self.to(base + p, place(peer), src if same else src.at[peer], dst.at[me])

        def start():
            @pl.loop(1, count)
            def _(p):
                copy(p).start()

        def finish():
            @pl.loop(1, count)
            def _(p):
                copy(p).wait()

        return start, finish


def sems(count):
    return [pltpu.SemaphoreType.DMA((count,)), pltpu.SemaphoreType.DMA((count,)), pltpu.SemaphoreType.DMA((8,))]


def anywhere():
    return pl.BlockSpec(memory_space=pl.ANY)


def comm_call(kernel, name, number, count, out_shape, args, in_specs=None, out_specs=None, scratch=()):
    return pl.pallas_call(
        kernel,
        out_shape=out_shape,
        in_specs=in_specs or [anywhere()] * len(args),
        out_specs=out_specs or [anywhere()] * len(out_shape),
        scratch_shapes=list(scratch) + sems(count),
        compiler_params=pltpu.CompilerParams(
            collective_id=number, has_side_effects=True, vmem_limit_bytes=40 * 1024 * 1024
        ),
        cost_estimate=pl.CostEstimate(flops=10**6, bytes_accessed=2**24, transcendentals=0),
        name=name,
    )(*args)


def b16(*shape):
    return jax.ShapeDtypeStruct(shape, BF16)


def gather_kernel(
    grad, weight, prod, filt, head,
    own_out, pair_out, prod_out, filt_out, top_out, head_out, send, recv, local,
):
    here = Here()
    links = Links(send, recv, local)
    x, w, y, c = here.x, here.w, here.y, here.c
    here.meet()
    right = links.to(0, here.along_x(1), grad, own_out.at[x])
    left = links.to(1, here.along_x(3), grad, own_out.at[x])
    share = links.to(2, here.across_w(), weight.at[c, y], pair_out.at[w, c, y])
    prods = links.pairs(16, 32, here.ctx, here.at_ctx, prod, prod_out)
    filts = links.pairs(48, 8, here.dp, here.at_dp, filt, filt_out, same=True)
    top = links.to(3, here.across_w(), grad.at[pl.ds(0, 64)], top_out)
    heads = links.to(4, here.before(), head, head_out)
    right.start()
    left.start()
    share.start()
    prods[0]()
    filts[0]()
    top.start()
    heads.start()
    locals_ = [
        links.own(0, grad, own_out.at[x]),
        links.own(1, weight, pair_out.at[w]),
        links.own(2, prod.at[here.ctx], prod_out.at[here.ctx]),
        links.own(3, filt, filt_out.at[here.dp]),
    ]
    for copy in locals_:
        copy.start()

    def piece(row, part=None):
        ref = pair_out.at[1 - w, c, row]
        return ref if part is None else ref.at[pl.ds(32 * part, 32)]

    def pass_on(n, place, row, part=None):
        copy = links.to(n, place, piece(row, part), piece(row, part))
        copy.start()
        return copy

    behind, ahead, far = lax.rem(y + 3, 4), lax.rem(y + 1, 4), lax.rem(y + 2, 4)
    share.wait_recv()
    up = pass_on(5, here.along_y(1), y)
    down = pass_on(6, here.along_y(3), y)
    over = [pass_on(7, here.across_c(), y)]
    up.wait_recv()
    up_half = pass_on(8, here.along_y(1), behind, 0)
    over.append(pass_on(9, here.across_c(), behind))
    down.wait_recv()
    down_half = pass_on(10, here.along_y(3), ahead, 1)
    over.append(pass_on(11, here.across_c(), ahead))

    x_behind, x_ahead = lax.rem(x + 3, 4), lax.rem(x + 1, 4)
    right.wait_recv()
    first = own_out.at[x_behind, pl.ds(0, 64)]
    right_half = links.to(12, here.along_x(1), first, first)
    right_half.start()
    left.wait_recv()
    second = own_out.at[x_ahead, pl.ds(64, 64)]
    left_half = links.to(13, here.along_x(3), second, second)
    left_half.start()
    up_half.wait_recv()
    down_half.wait_recv()
    over.append(pass_on(14, here.across_c(), far))
    prods[1]()
    filts[1]()
    for copy in over:
        copy.wait()
    for copy in (right_half, left_half, top, heads):
        copy.wait()
    for copy in (right, left, share, up, down, up_half, down_half):
        copy.wait_send()
    for copy in locals_:
        copy.wait()


def ring_steps(links, here, base, block, out):
    x = here.x
    half = block.shape[0] // 2
    right = links.to(base, here.along_x(1), block, out.at[x])
    left = links.to(base + 1, here.along_x(3), block, out.at[x])
    mine = links.own(7, block, out.at[x])
    first = out.at[lax.rem(x + 3, 4), pl.ds(0, half)]
    second = out.at[lax.rem(x + 1, 4), pl.ds(half, half)]
    right_half = links.to(base + 2, here.along_x(1), first, first)
    left_half = links.to(base + 3, here.along_x(3), second, second)

    def begin():
        right.start()
        left.start()
        mine.start()

    def forward():
        right.wait_recv()
        right_half.start()
        left.wait_recv()
        left_half.start()

    def finish():
        right_half.wait()
        left_half.wait()
        right.wait_send()
        left.wait_send()
        mine.wait()

    return begin, forward, finish


def middle_kernel(
    mix, filtered, grad, top, mix_out, filtered_out, bottom_out, ring_out, send, recv, local,
):
    here = Here()
    links = Links(send, recv, local)
    here.meet()
    mixes = links.pairs(0, 4, here.x, lambda i: (i, here.w, here.z, here.y, here.c), mix, mix_out)
    filts = links.pairs(16, 32, here.ctx, here.at_ctx, filtered, filtered_out)
    flip = links.to(4, here.across_w(), grad.at[pl.ds(64, 64)], bottom_out)
    ring = ring_steps(links, here, 5, top, ring_out)
    mixes[0]()
    filts[0]()
    ring[0]()
    flip.start()
    own = [
        links.own(0, mix.at[here.x], mix_out.at[here.x]),
        links.own(1, filtered.at[here.ctx], filtered_out.at[here.ctx]),
    ]
    for copy in own:
        copy.start()
    ring[1]()
    mixes[1]()
    filts[1]()
    flip.wait()
    ring[2]()
    for copy in own:
        copy.wait()


def spread_kernel(
    grad, mixed, bottom, mix_grad, filtered,
    grad_out, mixed_out, ring_out, mix_next_out, filtered_next_out, send, recv, local,
):
    here = Here()
    links = Links(send, recv, local)
    here.meet()
    grads = links.pairs(16, 32, here.ctx, here.at_ctx, grad, grad_out)
    mixes = links.pairs(48, 8, here.dp, here.at_dp, mixed, mixed_out)
    ring = ring_steps(links, here, 0, bottom, ring_out)
    nexts = [
        links.to(4, here.before(), mix_grad.at[:, pl.ds(0, 16)], mix_next_out),
        links.to(5, here.before(), filtered.at[:, pl.ds(0, 16)], filtered_next_out),
    ]
    grads[0]()
    mixes[0]()
    ring[0]()
    for copy in nexts:
        copy.start()
    own = [
        links.own(0, grad.at[here.ctx], grad_out.at[here.ctx]),
        links.own(1, mixed.at[here.dp], mixed_out.at[here.dp]),
    ]
    for copy in own:
        copy.start()
    ring[1]()
    mixes[1]()
    grads[1]()
    ring[2]()
    for copy in nexts + own:
        copy.wait()


def return_kernel(
    prod_grad, filt_grad, term,
    prod_out, filt_out, next_out, rows_out, half_ref, sum_ref, send, recv, local,
):
    here = Here()
    links = Links(send, recv, local)
    here.meet()
    half = links.to(0, here.across_c(), term.at[1 - here.c], half_ref)
    half.start()
    prods = links.pairs(16, 32, here.ctx, here.at_ctx, prod_grad, prod_out)
    filts = links.pairs(48, 8, here.dp, here.at_dp, filt_grad, filt_out)
    prods[0]()
    filts[0]()
    own = [
        links.own(0, prod_grad.at[here.ctx], prod_out.at[here.ctx]),
        links.own(1, filt_grad.at[here.dp], filt_out.at[here.dp]),
    ]
    for copy in own:
        copy.start()
    half.wait()

    @pl.loop(0, 16)
    def _(i):
        y, z = i // 4, lax.rem(i, 4)
        both = term[here.c, y, z].astype(F32) + half_ref[y, z].astype(F32)
        sum_ref[y, z] = both.astype(BF16)

    rows = links.pairs(8, 4, here.y, lambda i: (here.x, here.w, here.z, i, here.c), sum_ref, rows_out)
    rows[0]()
    mine = links.own(2, sum_ref.at[here.y], rows_out.at[here.y])
    mine.start()
    prods[1]()
    own[0].wait()
    ahead = links.to(1, here.before(), prod_out.at[:, pl.ds(0, 16)], next_out)
    ahead.start()
    filts[1]()
    rows[1]()
    ahead.wait()
    own[1].wait()
    mine.wait()


def last_kernel(
    parts_ref, rows_ref, total_ref, proj_ref,
    first, second, third, sum_ref, got_ref, send, recv, local,
):
    here = Here()
    links = Links(send, recv, local)
    here.meet()
    scatter = links.pairs(0, 32, here.ctx, here.at_ctx, parts_ref, first)
    share = links.pairs(32, 8, here.dp, here.at_dp, second.at[here.dp], second, same=True)
    gather = links.pairs(40, 32, here.ctx, here.at_ctx, third.at[here.ctx], third, same=True)
    zs = links.pairs(72, 4, here.z, lambda i: (here.x, here.w, i, here.y, here.c), sum_ref, got_ref)
    scatter[0]()
    first[here.ctx] = parts_ref[here.ctx]

    @pl.loop(0, 4)
    def _(z):
        total = rows_ref[0, z].astype(F32)
        for y in range(1, 4):
            total = total + rows_ref[y, z].astype(F32)
        sum_ref[z] = total.astype(BF16)

    zs[0]()
    got_ref[here.z] = sum_ref[here.z]
    scatter[1]()
    second[here.dp] = jnp.sum(first[...], axis=0)
    share[0]()
    share[1]()
    third[here.ctx] = jnp.sum(second[...], axis=0)
    gather[0]()
    zs[1]()
    total = got_ref[0].astype(F32)
    for z in range(1, 4):
        total = total + got_ref[z].astype(F32)
    proj_ref[...] = total * GRAD_SCALE
    gather[1]()
    total_ref[...] = third[...] * GRAD_SCALE


def weight_kernel(mixed_ref, own_ref, top_ref, bottom_ref, out_ref):
    rest = jnp.concatenate([top_ref[...], bottom_ref[...]], 0)
    total = dot32(mixed_ref[:, :512], own_ref[...]) + dot32(mixed_ref[:, 512:], rest)
    total = total.astype(BF16)
    for z in range(4):
        for y in range(4):
            for c in range(2):
                at = (z * 8 + y * 2 + c) * 16
                out_ref[c, y, z] = total[at : at + 16]


def weight_term_of(mixed, own, top, bottom):
    return pl.pallas_call(
        weight_kernel,
        grid=(8,),
        out_shape=jax.ShapeDtypeStruct((2, 4, 4, 16, 4096), BF16),
        in_specs=[pl.BlockSpec((512, 1024), lambda i: (0, 0)), flat_spec(512), flat_spec(256), flat_spec(256)],
        out_specs=pl.BlockSpec((2, 4, 4, 16, WIDE), lambda i: (0, 0, 0, 0, i)),
        compiler_params=pltpu.CompilerParams(vmem_limit_bytes=32 * 1024 * 1024),
        cost_estimate=pl.CostEstimate(flops=2**32, bytes_accessed=13 * 2**20, transcendentals=0),
        name="weight_term",
    )(mixed, own, top, bottom)


def body(streams, out_grad, proj_weight, long_filter, short_taps, doc_ids):
    rows = streams.shape[1]
    first_row = ((lax.axis_index(DP) * 32) + lax.axis_index(CTX)) * rows
    edge_ids = jnp.full((2,), -1, jnp.int32)
    id_rows = lax.dynamic_slice_in_dim(jnp.concatenate([edge_ids, doc_ids, edge_ids]), first_row, rows + 4)
    own_ids = id_rows[2 : 2 + rows]
    place = lax.axis_index(CTX) * rows + jnp.arange(rows)
    near = [
        jnp.logical_and(id_rows[2 + d : 2 + d + rows] == own_ids, jnp.logical_and(place + d >= 0, place + d < LENGTH))
        for d in (-1, -2, 1, 2)
    ]
    masks = jnp.stack(near + [jnp.zeros((rows,), bool)] * 4, axis=1).astype(F32)
    early = step_along(streams[:, rows - 2 :, :], CTX, 1)
    tables = tables_in()
    query, prod, head = short_filter(streams, early, short_taps, masks)
    own_groups, pair, prod_chan, filt, top, head_next = comm_call(
        gather_kernel, "gather", 1, 56,
        [b16(4, rows, 4096), b16(2, 2, 4, 64, 4096), b16(32, STEP, STEP), b16(8, 512, STEP), b16(64, 4096),
         jax.ShapeDtypeStruct((2, 8, 4096), F32)],
        (out_grad, proj_weight.reshape(2, 4, 64, 4096), prod, long_filter.astype(BF16), head),
    )
    own_groups = own_groups.reshape(512, 4096)
    mix_grad_groups = lax.dot_general(
        own_groups, pair.reshape(1024, 4096), (((1,), (1,)), ((), ())), preferred_element_type=F32
    ).astype(BF16)
    filtered_chan, spec_prod, spec_filt = filter_forward(prod_chan, filt.reshape(32, STEP, STEP), tables)
    mix_grad, filtered, bottom, top_ring = comm_call(
        middle_kernel, "middle", 2, 48,
        [b16(4, rows, 1024), b16(32, STEP, STEP), b16(64, 4096), b16(4, 64, 4096)],
        (mix_grad_groups.reshape(4, rows, 1024), filtered_chan, out_grad, top),
    )
    filtered_grad_chan, mixed, bottom_ring, mix_next, filtered_next = comm_call(
        spread_kernel, "spread", 3, 56,
        [b16(32, STEP, STEP), b16(8, rows, WIDE), b16(4, 64, 4096), b16(4, 16, 1024), b16(32, 16, STEP)],
        (filtered_grad_of(mix_grad, query), mixed_of(query, filtered), bottom, mix_grad, filtered),
    )
    w = lax.axis_index("w")
    mixed = mixed.reshape(4, 2, rows, WIDE)
    mixed = jnp.where(w == 0, mixed, mixed[:, ::-1])
    mixed_flip = mixed[:, 1].reshape(4, 2, 64, WIDE).transpose(1, 0, 2, 3).reshape(512, WIDE)
    mixed = jnp.concatenate([mixed[:, 0].reshape(512, WIDE), mixed_flip], 0).T
    weight_term = weight_term_of(mixed, own_groups, top_ring.reshape(256, 4096), bottom_ring.reshape(256, 4096))
    prod_grad_chan, filt_term = filter_backward(filtered_grad_chan, spec_prod, spec_filt, tables)
    prod_grad, filt_parts, prod_next, row_parts = comm_call(
        return_kernel, "returned", 4, 56,
        [b16(32, STEP, STEP), b16(8, 512, STEP), b16(32, 16, STEP), b16(4, 4, 16, 4096)],
        (prod_grad_chan, filt_term.reshape(8, 512, STEP), weight_term),
        in_specs=[anywhere(), anywhere(), vmem()],
        scratch=[pltpu.VMEM((4, 4, 16, 4096), BF16)] * 2,
    )
    stream_grads, tap_parts = final_grads(
        streams, early, short_taps, masks, mix_grad, filtered, prod_grad,
        (mix_next, filtered_next, prod_next, head_next),
    )
    filter_grad = jnp.sum(filt_parts.astype(F32), axis=0) * GRAD_SCALE
    taps, proj_grad = comm_call(
        last_kernel, "last", 5, 76,
        [jax.ShapeDtypeStruct((32, 16, STEP), F32), jax.ShapeDtypeStruct((16, 4096), F32)],
        (tap_parts, row_parts),
        in_specs=[vmem(), vmem()], out_specs=[vmem(), vmem()],
        scratch=[
            pltpu.VMEM((32, 16, STEP), F32), pltpu.VMEM((8, 16, STEP), F32), pltpu.VMEM((32, 16, STEP), F32),
            pltpu.VMEM((4, 16, 4096), BF16), pltpu.VMEM((4, 16, 4096), BF16),
        ],
    )
    tap_grad = taps[:, :9, :].transpose(1, 0, 2).reshape(3, 3, 4096)
    return stream_grads, proj_grad, filter_grad, tap_grad


def solution(mesh):
    devices = np.asarray(mesh.devices).reshape(4, 2, 4, 4, 2)
    fine = Mesh(devices, ("x", "w", "z", "y", "c"))
    every = DP + CTX
    return jax.shard_map(
        body,
        mesh=fine,
        in_specs=(P(None, every, None), P(every, None), P(DP, None), P(DP, CTX), P(), P()),
        out_specs=(P(None, every, None), P(every, None), P(DP, CTX), P()),
        check_vma=False,
    )
```

time: 1030 us -> 357 us (0.35); the launches traced: 1010 us -> 356 us
  waiting for transfers between devices: 590 us -> 0.01 us
  Pallas kernels: 0 us -> 305 us
  other arithmetic: 145 us -> 3.9 us
  local copies, waits for them, and re-layouts: 136 us -> 32.2 us
  matrix products: 74.1 us -> 8.7 us
  starting transfers between devices: 51.5 us -> 4.59 us
  between operations: 15 us -> 1.07 us
    pallas_call x0 -> x12, Pallas kernels: none -> 305 us  [the longest x5 244 us: comm_call(): pl.pallas_call(kernel, out_shape=out_shape, in_specs=in_specs or [anywher...]
    psum x1 -> x0, waiting for transfers between devices: 230 us -> none  [body(): tap_grad = lax.psum(jnp.stack(tap_terms), ('dp', 'ctx')) * grad_scale]
    all_gather x2 -> x0, waiting for transfers between devices: 201 us -> none  [the longest x1 153 us: projection_grads(): gathered = lax.all_gather(out_grad, 'dp', axis=0, tiled=True)]
    reduce_scatter x2 -> x0, waiting for transfers between devices: 98.9 us -> none  [the longest x1 98.9 us: body(): lax.psum_scatter(weight_term.astype(jnp.bfloat16), 'ctx', scatter_dimensi...]
    slice x15 -> x2, local copies, waits for them, and re-layouts: 95.4 us -> 1.95 us  [the longest x1 1.07 us: body(): early = step_along(streams[:, rows - 2:, :], CTX, 1)]
    dot_general x10 -> x1, matrix products: 74.1 us -> 8.7 us  [body(): lax.dot_general(own_groups, pair.reshape(1024, 4096), (((1,), (1,)), ((),...]
    all_to_all x6 -> x0, waiting for transfers between devices: 59.6 us -> none  [the longest x1 28.8 us: body(): lax.all_to_all(product_grad_chan.astype(jnp.bfloat16), 'ctx', split_axis=...]
    all_to_all x6 -> x0, starting transfers between devices: 44.8 us -> none  [the longest x1 11.3 us: body(): lax.all_to_all(filtered_grad, 'ctx', split_axis=1, concat_axis=0, tiled=T...]
  transfers between devices with their start and end apart: 13 -> 1, of which waited for: 7 -> 0; matrix products, arithmetic and copies ran while one was open for 14% -> 1% of each run, Pallas kernels for 0% -> 0%
where the time goes in v1:
time: 357 us; the launch traced here: 356 us
  Pallas kernels  305 us (85%)
  local copies, waits for them, and re-layouts  32.2 us (9%)
  matrix products  8.7 us (2%)
  starting transfers between devices  4.59 us (1%)
  other arithmetic  3.9 us (1%)
    pallas_call x5, Pallas kernels, comm_call(): pl.pallas_call(kernel, out_shape=out_shape, in_specs=in_specs or [anywher...  244 us
    unnamed x71, local copies, waits for them, and re-layouts  23.1 us
    pallas_call x1, Pallas kernels, final_grads(): pl.pallas_call(final_kernel, grid=(8,), out_shape=[jax.ShapeDtypeStruct((...  13.3 us
    pallas_call x1, Pallas kernels, filter_forward(): pl.pallas_call(filter_forward_kernel, out_shape=[jax.ShapeDtypeStruct((32...  11.7 us
    pallas_call x1, Pallas kernels, filter_backward(): pl.pallas_call(filter_backward_kernel, out_shape=[out, out], in_specs=[vm...  10.4 us
    dot_general x1, matrix products, body(): lax.dot_general(own_groups, pair.reshape(1024, 4096), (((1,), (1,)), ((),...  8.7 us
    pallas_call x1, Pallas kernels, short_filter(): pl.pallas_call(short_kernel, grid=(8,), out_shape=[jax.ShapeDtypeStruct((...  7.53 us
  transfers between devices with their start and end apart: 1, of which 0 were waited for; matrix products, arithmetic and copies ran while one was open for 1% of the time, Pallas kernels for 0%

profile of v1, /device:TPU:1, one launch (start us, length us, event | category | flops | bytes accessed | tf_op | source)
XLA Modules:
  0.0 355.7 jit_solution(15796193935893200905)
XLA Ops:
  0.6 1.1 slice.27
  1.7 4.6 %collective-permute-start = (bf16[3,2,4096]{2,1,0:T(2,128)(2,1)S(1)}, bf16[3,2,4096]{2,1,0:T(2,128)(2,1)S(1)}, u32[]{:S(2)}, u32[]{:S(2)}) collective-permute-start(bf16[3,2,4096]{2,1,0:T(2,128)(2,1)S(1)} %slice.27), channel_id=1, source_target_pairs={{0,1},{1,2},{2,3},{3,4},{4,5},{5,6},{6,7},{7,8},{8,9},{9,10},{10,1... | collective-permute-start | bytes 147464 | tf_op jit(solution)/shard_map/ppermute | solution.py:393
  6.3 1.0 concatenate.6
  7.5 1.0 convert_element_type.13.filt
  8.6 0.1 copy.31
  8.7 0.6 convert_element_type.12.masks_ref
  9.3 0.6 copy-done.33
  9.9 7.5 %short_filter.1 = (bf16[128,4096]{1,0:T(8,128)(2,1)}, bf16[32,128,128]{2,1,0:T(8,128)(2,1)}, f32[2,8,4096]{2,1,0:T(8,128)}) custom-call(bf16[3,128,4096]{2,1,0:T(8,128)(2,1)} %streams_ref.3, bf16[3,2,4096]{2,1,0:T(2,128)(2,1)} %copy-done.33, f32[3,3,4096]{2,1,0:T(4,128)} %taps_ref.3, f32[128,8]{1,0:T(8,128)} %convert_element_type.12.masks_ref), custom_call_target="tpu_custom_call" | custom-call | flops 10000000 | bytes 5242880 | tf_op jit(solution)/shard_map/short_filter/pallas_call | solution.py:279
  17.5 2.2 copy-done.5
  19.7 1.2 copy-done.9
  20.9 0.9 copy-done.12
  21.8 73.4 %gather.1 = (bf16[4,128,4096]{2,1,0:T(8,128)(2,1)S(1)}, bf16[2,2,4,64,4096]{4,3,2,1,0:T(8,128)(2,1)}, bf16[32,128,128]{2,1,0:T(8,128)(2,1)S(1)}, bf16[8,512,128]...) custom-call(bf16[128,4096]{1,0:T(8,128)(2,1)S(1)} %copy-done.4, ...), custom_call_target="tpu_custom_call" | custom-call | flops 1000000 | bytes 16777216 | tf_op jit(solution)/shard_map/gather/pallas_call | solution.py:482
  95.3 8.7 %convolution_convert_fusion = bf16[512,1024]{1,0:T(8,128)(2,1)S(1)} fusion(bf16[512,4096]{1,0:T(8,128)(2,1)S(1)} %bitcast.32, bf16[1024,4096]{1,0:T(8,128)(2,1)} %bitcast.40), kind=kOutput, calls=%fused_computation.2 | convolution fusion | flops 4295491584 | bytes 13631488 | tf_op jit(solution)/shard_map/dot_general | solution.py:796
  104.1 2.6 broadcast_in_dim.2.twist_ref
  106.7 11.7 %filter_forward.1 = (bf16[32,128,128]{2,1,0:T(8,128)(2,1)S(1)}, f32[32,256,128]{2,1,0:T(8,128)S(1)}, f32[32,256,128]{2,1,0:T(8,128)S(1)}) custom-call(bf16[32,128,128]{2,1,0:T(8,128)(2,1)S(1)} %get-tuple-element.39.prod_ref, bf16[32,128,128]{2,1,0:T(8,128)(2,1)S(1)} %bitcast.36, bf16[512,256]{1,0:T(8,128)(2,1)S(1)} %copy-done.27, ...), custom_call_target="tpu_custom_call" | custom-call | flops 12000000000 | bytes 18874368 | tf_op jit(solution)/shard_map/filter_forward/pallas_call | solution.py:202
  118.4 2.0 copy-done.29
  120.4 1.9 copy-done.31
  122.3 40.7 %middle.1 = (bf16[4,128,1024]{2,1,0:T(8,128)(2,1)S(1)}, bf16[32,128,128]{2,1,0:T(8,128)(2,1)S(1)}, bf16[64,4096]{1,0:T(8,128)(2,1)S(1)}, bf16[4,64,4096]{2,1,0:T(8,128)(2,1)S(1)}) custom-call(bf16[4,128,1024]{2,1,0:T(8,128)(2,1)S(1)} %bitcast.29, bf16[32,128,128]{2,1,0:T(8,128)(2,1)S(1)} %get-tuple-element.41.filtered, bf16[128,4096]{1,0:T(8,128)(2,1)S(1)} %copy-done.4, ...), custom_call_target="tpu_custom_call" | custom-call | flops 1000000 | bytes 16777216 | tf_op jit(solution)/shard_map/middle/pallas_call | solution.py:482
  163.1 1.0 copy-done
  164.1 1.0 copy-done.2
  165.1 1.3 copy-done.18
  166.4 5.7 %filtered_grad.1.grad = bf16[32,128,128]{2,1,0:T(8,128)(2,1)} custom-call(bf16[4,128,1024]{2,1,0:T(8,128)(2,1)} %copy-done, bf16[128,4096]{1,0:T(8,128)(2,1)} %get-tuple-element.45.query_ref), custom_call_target="tpu_custom_call" | custom-call | flops 1000000 | bytes 3145728 | tf_op jit(solution)/shard_map/filtered_grad/pallas_call | solution.py:319
  172.1 5.6 %mixed.1 = bf16[8,128,512]{2,1,0:T(8,128)(2,1)} custom-call(bf16[128,4096]{1,0:T(8,128)(2,1)} %get-tuple-element.45.query_ref, bf16[32,128,128]{2,1,0:T(8,128)(2,1)} %copy-done.2), custom_call_target="tpu_custom_call" | custom-call | flops 1000000 | bytes 3145728 | tf_op jit(solution)/shard_map/mixed/pallas_call | solution.py:301
  177.7 1.2 copy-done.6
  178.9 1.2 copy-done.7
  180.1 44.9 %spread.1 = (bf16[32,128,128]{2,1,0:T(8,128)(2,1)S(1)}, bf16[8,128,512]{2,1,0:T(8,128)(2,1)S(1)}, bf16[4,64,4096]{2,1,0:T(8,128)(2,1)S(1)}, bf16[4,16,1024]{2,1,0:T(8,128)(2,1)S(1)}, bf16[32,16,128]{2,1,0:T(8,128)(2,1)S(1)}) custom-call(bf16[32,128,128]{2,1,0:T(8,128)(2,1)S(1)} %copy-done.6, bf16[8,128,512]{2,1,0:T(8,128)(2,1)S(1)} %copy-done.7, ...), custom_call_target="tpu_custom_call" | custom-call | flops 1000000 | bytes 16777216 | tf_op jit(solution)/shard_map/spread/pallas_call | solution.py:482
  225.1 0.5 copy-done.13
  225.7 0.2 reverse_select_fusion
  225.9 0.9 fusion
  226.8 0.2 copy-done.22
  227.0 0.2 copy.38
  227.2 1.2 copy.35
  228.4 1.0 copy.36
  229.4 1.1 maximum_bitcast_fusion.mixed_ref
  230.6 2.2 copy-done.30
  232.7 2.2 copy-done.32
  234.9 10.4 %filter_backward.1 = (bf16[32,128,128]{2,1,0:T(8,128)(2,1)S(1)}, bf16[32,128,128]{2,1,0:T(8,128)(2,1)S(1)}) custom-call(bf16[32,128,128]{2,1,0:T(8,128)(2,1)S(1)} %copy-done.23, f32[32,256,128]{2,1,0:T(8,128)S(1)} %copy-done.30, f32[32,256,128]{2,1,0:T(8,128)S(1)} %copy-done.32, bf16[512,256]{1,0:T(8,128)(2,1)S(1)} %copy-done.28, ...), custom_call_target="tpu_custom_call" | custom-call | flops 12000000000 | bytes 18874368 | tf_op jit(solution)/shard_map/filter_backward/pallas_call | solution.py:216
  245.4 6.6 %weight_term.1.term = bf16[2,4,4,16,4096]{4,3,2,1,0:T(8,128)(2,1)S(1)} custom-call(bf16[512,1024]{1,0:T(8,128)(2,1)S(1)} %maximum_bitcast_fusion.mixed_ref, bf16[512,4096]{1,0:T(8,128)(2,1)S(1)} %bitcast.33, bf16[256,4096]{1,0:T(8,128)(2,1)S(1)} %bitcast.34, bf16[256,4096]{1,0:T(8,128)(2,1)S(1)} %bitcast.35), custom_call_target="tpu_custom_call" | custom-call | flops 4294967296 | bytes 13631488 | tf_op jit(solution)/shard_map/weight_term/pallas_call | solution.py:762
  252.0 43.9 %returned.1 = (bf16[32,128,128]{2,1,0:T(8,128)(2,1)S(1)}, bf16[8,512,128]{2,1,0:T(8,128)(2,1)S(1)}, bf16[32,16,128]{2,1,0:T(8,128)(2,1)S(1)}, bf16[4,4,16,4096]{3,2,1,0:T(8,128)(2,1)S(1)}) custom-call(bf16[32,128,128]{2,1,0:T(8,128)(2,1)S(1)} %get-tuple-element.50.prod_grad, bf16[8,512,128]{2,1,0:T(8,128)(2,1)S(1)} %bitcast.31, ...), custom_call_target="tpu_custom_call" | custom-call | flops 1000000 | bytes 16777216 | tf_op jit(solution)/shard_map/returned/pallas_call | solution.py:482
  295.9 1.0 copy-done.8
  296.9 0.7 copy-done.15
  297.5 13.3 %final_grads.1 = (bf16[3,128,4096]{2,1,0:T(8,128)(2,1)}, f32[32,16,128]{2,1,0:T(8,128)}) custom-call(bf16[3,128,4096]{2,1,0:T(8,128)(2,1)} %streams_ref.3, bf16[3,2,4096]{2,1,0:T(2,128)(2,1)} %copy-done.33, f32[3,3,4096]{2,1,0:T(4,128)} %taps_ref.3, f32[128,8]{1,0:T(8,128)} %convert_element_type.12.masks_ref, bf16[4,128,1024]{2,1,0:T(8,128)(2,1)} %copy-done, ...), custom_call_target="tpu_custom_call" | custom-call | flops 30000000 | bytes 9437184 | tf_op jit(solution)/shard_map/final_grads/pallas_call | solution.py:373
  310.8 0.9 copy-done.11
  311.8 41.5 %last.1 = (f32[32,16,128]{2,1,0:T(8,128)S(1)}, f32[16,4096]{1,0:T(8,128)S(1)}) custom-call(f32[32,16,128]{2,1,0:T(8,128)S(1)} %copy-done.11, bf16[4,4,16,4096]{3,2,1,0:T(8,128)(2,1)S(1)} %get-tuple-element.62.rows_ref), custom_call_target="tpu_custom_call" | custom-call | flops 1000000 | bytes 16777216 | tf_op jit(solution)/shard_map/last/pallas_call | solution.py:482
  353.4 0.7 reshape.52
  354.1 0.1 convert_reduce_fusion
  354.3 0.7 broadcast_multiply_fusion
  355.0 0.7 copy.40
  (61 shorter events, 0.5 us)
Async XLA Ops:
  0.6 16.8 %copy-start.4 = (bf16[128,4096]{1,0:T(8,128)(2,1)S(1)}, bf16[128,4096]{1,0:T(8,128)(2,1)}, u32[]{:S(2)}) copy-start(bf16[128,4096]{1,0:T(8,128)(2,1)} %grad.3) | copy-start | bytes 3145732
  1.7 7.6 %collective-permute-start = (bf16[3,2,4096]{2,1,0:T(2,128)(2,1)S(1)}, bf16[3,2,4096]{2,1,0:T(2,128)(2,1)S(1)}, u32[]{:S(2)}, u32[]{:S(2)}) collective-permute-start(bf16[3,2,4096]{2,1,0:T(2,128)(2,1)S(1)} %slice.27), channel_id=1, source_target_pairs={{0,1},{1,2},{2,3},{3,4},{4,5},{5,6},{6,7},{7,8},{8,9},{9,10},{10,1... | collective-permute-start | bytes 147464 | tf_op jit(solution)/shard_map/ppermute | solution.py:393
  9.3 0.6 copy-start.33
  17.5 2.2 copy-start.5
  19.7 1.2 copy-start.9
  20.9 0.9 copy-start.12
  95.2 8.7 %copy-start.10 = (f32[2,8,4096]{2,1,0:T(8,128)}, f32[2,8,4096]{2,1,0:T(8,128)S(1)}, u32[]{:S(2)}) copy-start(f32[2,8,4096]{2,1,0:T(8,128)S(1)} %get-tuple-element.59.head_next_ref) | copy-start | bytes 786436
  95.2 8.7 %copy-start.16 = (bf16[4,128,4096]{2,1,0:T(8,128)(2,1)}, bf16[4,128,4096]{2,1,0:T(8,128)(2,1)S(1)}, u32[]{:S(2)}) copy-start(bf16[4,128,4096]{2,1,0:T(8,128)(2,1)S(1)} %get-tuple-element.37) | copy-start | bytes 12582916
  95.3 8.8 %copy-start.34 = (f32[32,256]{1,0:T(8,128)S(1)}, f32[32,256]{1,0:T(8,128)}, u32[]{:S(2)}) copy-start(f32[32,256]{1,0:T(8,128)} %constant.58.clone) | copy-start | bytes 98308
  104.0 2.7 copy-start.24
  104.0 2.6 copy-start.25
  104.0 2.6 copy-start.26
  104.0 2.6 copy-start.27
  118.4 2.0 copy-start.29
  120.4 1.9 copy-start.31
  163.1 1.0 copy-start
  164.1 1.0 copy-start.2
  165.1 1.3 copy-start.18
  166.4 11.3 %copy-start.1 = (bf16[4,128,1024]{2,1,0:T(8,128)(2,1)S(1)}, bf16[4,128,1024]{2,1,0:T(8,128)(2,1)}, u32[]{:S(2)}) copy-start(bf16[4,128,1024]{2,1,0:T(8,128)(2,1)} %copy-done) | copy-start | bytes 3145732
  166.4 11.3 %copy-start.3 = (bf16[32,128,128]{2,1,0:T(8,128)(2,1)S(1)}, bf16[32,128,128]{2,1,0:T(8,128)(2,1)}, u32[]{:S(2)}) copy-start(bf16[32,128,128]{2,1,0:T(8,128)(2,1)} %copy-done.2) | copy-start | bytes 3145732
  177.7 1.2 copy-start.6
  178.9 1.2 copy-start.7
  225.0 0.7 copy-start.13
  225.0 0.8 copy-start.14
  225.0 1.7 copy-start.20
  225.0 1.9 copy-start.22
  225.9 4.6 %copy-start.28 = (bf16[512,256]{1,0:T(8,128)(2,1)S(1)}, bf16[512,256]{1,0:T(8,128)(2,1)}, u32[]{:S(2)}) copy-start(bf16[512,256]{1,0:T(8,128)(2,1)} %constant.59.clone.first_ref) | copy-start | bytes 786436
  227.0 3.6 %copy-start.23 = (bf16[32,128,128]{2,1,0:T(8,128)(2,1)S(1)}, bf16[32,128,128]{2,1,0:T(8,128)(2,1)}, u32[]{:S(2)}) copy-start(bf16[32,128,128]{2,1,0:T(8,128)(2,1)} %copy-done.22) | copy-start | bytes 3145732
  230.5 2.2 copy-start.30
  232.7 2.2 copy-start.32
  234.9 10.4 %copy-start.17 = (bf16[4,128,4096]{2,1,0:T(8,128)(2,1)S(1)}, bf16[4,128,4096]{2,1,0:T(8,128)(2,1)}, u32[]{:S(2)}) copy-start(bf16[4,128,4096]{2,1,0:T(8,128)(2,1)} %copy-done.16) | copy-start | bytes 12582916
  234.9 10.5 %copy-start.19 = (bf16[4,64,4096]{2,1,0:T(8,128)(2,1)S(1)}, bf16[4,64,4096]{2,1,0:T(8,128)(2,1)}, u32[]{:S(2)}) copy-start(bf16[4,64,4096]{2,1,0:T(8,128)(2,1)} %copy-done.18) | copy-start | bytes 6291460
  234.9 10.5 %copy-start.21 = (bf16[4,64,4096]{2,1,0:T(8,128)(2,1)S(1)}, bf16[4,64,4096]{2,1,0:T(8,128)(2,1)}, u32[]{:S(2)}) copy-start(bf16[4,64,4096]{2,1,0:T(8,128)(2,1)} %copy-done.20) | copy-start | bytes 6291460
  295.9 1.0 copy-start.8
  296.9 0.7 copy-start.15
  310.8 1.0 copy-start.11

commit v2 on v1

v2 whole, which is shorter than its diff:
```python
import functools
import math

import jax
import jax.numpy as jnp
import numpy as np
from jax import lax
from jax.experimental import pallas as pl
from jax.experimental.pallas import tpu as pltpu
from jax.sharding import Mesh
from jax.sharding import PartitionSpec as P

DP = ("x", "w")
CTX = ("z", "y", "c")
F32 = jnp.float32
BF16 = jnp.bfloat16
LENGTH = 4096
TOTAL = 2 * LENGTH
SLOTS = 32
STEP = 128
WIDE = 512
GRAD_SCALE = float(32768) ** (-0.5)
MESH = pl.DeviceIdType.MESH


def split_table(table):
    return table.astype(BF16)


def make_tables():
    a = np.arange(32)
    b = np.arange(STEP)
    first = np.zeros((2 * SLOTS, 32))
    first[0] = 1.0
    first[1] = (-1.0) ** a
    for s in range(1, SLOTS):
        first[2 * s] = np.cos(2 * np.pi * a * s / 64)
        first[2 * s + 1] = -np.sin(2 * np.pi * a * s / 64)
    first_wide = np.kron(first, np.eye(8))
    last_wide = np.kron(first.T * (2.0 / TOTAL), np.eye(8))
    angle = 2 * np.pi * np.outer(b, b) / STEP
    cosine, sine = np.cos(angle), np.sin(angle)
    plain = np.block([[cosine, sine], [-sine, cosine]])
    special = np.zeros((2 * STEP, 2 * STEP))
    half = np.arange(64)
    even = 2 * np.pi * np.outer(half, b) / STEP
    odd = 2 * np.pi * np.outer(32 + 64 * half, b) / TOTAL
    special[:64, :STEP] = np.cos(even)
    special[64:128, STEP:] = np.cos(odd)
    special[128:192, :STEP] = -np.sin(even)
    special[128, :STEP] = (-1.0) ** b
    special[192:, STEP:] = -np.sin(odd)
    middle = np.stack([split_table(special), split_table(plain)])
    middle_back = np.stack([split_table(special.T), split_table(plain.T)])
    turn = 2 * np.pi * np.outer(np.arange(SLOTS), b) / TOTAL
    twist = np.concatenate([np.cos(turn), np.sin(turn)], 1).astype(np.float32)
    return split_table(first_wide), split_table(last_wide), middle, middle_back, twist


def dot32(a, b):
    return jnp.dot(a, b, preferred_element_type=F32)


def dot16(table, value):
    return dot32(table, value.astype(BF16))


def twisted(re, im, c, s):
    return re * c + im * s, im * c - re * s


def untwisted(re, im, c, s):
    return re * c - im * s, im * c + re * s


def halves_of(block):
    return [block[:, :8, :].reshape(256, STEP), block[:, 8:, :].reshape(256, STEP)]


def edge_rows(k):
    rows = lax.broadcasted_iota(jnp.int32, (STEP, STEP), 0)
    return jnp.logical_and(rows == 0, k == 0)


def filter_forward_kernel(
    prod_ref, filt_ref, first_ref, last_ref, mid_ref, back_ref, twist_ref,
    out_ref, spec_prod_ref, spec_filt_ref, yp_ref, yf_ref,
):
    first = first_ref[...]

    @pl.loop(0, 8, unroll=2)
    def _(h):
        rows = pl.ds(pl.multiple_of(16 * h, 16), 16)
        prods = halves_of(prod_ref[:, rows, :].astype(F32))
        filts = halves_of(filt_ref[:, :, rows, :].reshape(32, 16, STEP).astype(F32))
        for j in range(2):
            wide = dot32(first, jnp.concatenate([prods[j], filts[j]], 1).astype(BF16))
            at = pl.ds(pl.multiple_of(16 * h + 8 * j, 8), 8)
            yp_ref[:, at, :] = wide[:, :128].reshape(64, 8, STEP)
            yf_ref[:, at, :] = wide[:, 128:].reshape(64, 8, STEP)

    @pl.loop(0, SLOTS, unroll=4)
    def _(k):
        c, s = twist_ref[k, :STEP, :], twist_ref[k, STEP:, :]
        which = jnp.minimum(k, 1)
        pair = pl.ds(2 * k, 2)
        yp, yf = yp_ref[pair], yf_ref[pair]
        pr, pi = twisted(yp[0], yp[1], c, s)
        fr, fi = twisted(yf[0], yf[1], c, s)
        value = jnp.concatenate([jnp.concatenate([pr, pi], 0), jnp.concatenate([fr, fi], 0)], 1)
        spec = dot16(mid_ref[which], value)
        spec_prod_ref[k] = spec[:, :128]
        spec_filt_ref[k] = spec[:, 128:]
        pr, pi = spec[:128, :128], spec[128:, :128]
        fr, fi = spec[:128, 128:], spec[128:, 128:]
        edge = edge_rows(k)
        re = jnp.where(edge, 0.5 * (pr * fr), pr * fr - pi * fi)
        im = jnp.where(edge, 0.5 * (pi * fi), pr * fi + pi * fr)
        back = dot16(back_ref[which], jnp.concatenate([re, im], 0))
        re, im = untwisted(back[:128], back[128:], c, s)
        yp_ref[2 * k] = re
        yp_ref[2 * k + 1] = im

    last = last_ref[...]

    @pl.loop(0, 8, unroll=2)
    def _(h):
        halves = [yp_ref[:, pl.ds(pl.multiple_of(16 * h + 8 * j, 8), 8), :].reshape(512, STEP) for j in range(2)]
        out = dot16(last, jnp.concatenate(halves, 1))
        parts = [out[:, 128 * j : 128 * (j + 1)].reshape(32, 8, STEP) for j in range(2)]
        rows = pl.ds(pl.multiple_of(16 * h, 16), 16)
        out_ref[:, rows, :] = jnp.concatenate(parts, 1).astype(BF16)


def filter_backward_kernel(
    grad_ref, spec_prod_ref, spec_filt_ref, first_ref, last_ref, mid_ref, back_ref, twist_ref,
    prod_grad_ref, filt_grad_ref, yg_ref, yv_ref,
):
    first = first_ref[...]

    @pl.loop(0, 8, unroll=2)
    def _(h):
        rows = pl.ds(pl.multiple_of(16 * h, 16), 16)
        grads = halves_of(grad_ref[:, rows, :].astype(F32))
        grad = jnp.concatenate([grads[0], grads[1]], 1).astype(BF16)
        out = dot32(first, grad)
        for j in range(2):
            at = pl.ds(pl.multiple_of(16 * h + 8 * j, 8), 8)
            yg_ref[:, at, :] = out[:, 128 * j : 128 * (j + 1)].reshape(64, 8, STEP)

    @pl.loop(0, SLOTS, unroll=4)
    def _(k):
        c, s = twist_ref[k, :STEP, :], twist_ref[k, STEP:, :]
        which = jnp.minimum(k, 1)
        yg = yg_ref[pl.ds(2 * k, 2)]
        gr, gi = twisted(yg[0], yg[1], c, s)
        spec = dot16(mid_ref[which], jnp.concatenate([gr, gi], 0))
        gr, gi = spec[:128], spec[128:]
        edge = edge_rows(k)
        cols = []
        for ref in (spec_filt_ref, spec_prod_ref):
            hr, hi = ref[k, :STEP, :], ref[k, STEP:, :]
            re = jnp.where(edge, 0.5 * (hr * gr), hr * gr + hi * gi)
            im = jnp.where(edge, 0.5 * (hi * gi), hr * gi - hi * gr)
            cols.append(jnp.concatenate([re, im], 0))
        back = dot16(back_ref[which], jnp.concatenate(cols, 1))
        re, im = untwisted(back[:128, :128], back[128:, :128], c, s)
        yg_ref[2 * k] = re
        yg_ref[2 * k + 1] = im
        re, im = untwisted(back[:128, 128:], back[128:, 128:], c, s)
        yv_ref[2 * k] = re
        yv_ref[2 * k + 1] = im

    last = last_ref[...]

    @pl.loop(0, 8, unroll=2)
    def _(h):
        parts, other = [], []
        for j in range(2):
            at = pl.ds(pl.multiple_of(16 * h + 8 * j, 8), 8)
            value = jnp.concatenate([yg_ref[:, at, :].reshape(512, STEP), yv_ref[:, at, :].reshape(512, STEP)], 1)
            out = dot16(last, value)
            parts.append(out[:, :128].reshape(32, 8, STEP))
            other.append(out[:, 128:].reshape(32, 8, STEP))
        rows = pl.ds(pl.multiple_of(16 * h, 16), 16)
        prod_grad_ref[:, rows, :] = jnp.concatenate(parts, 1).astype(BF16)
        filt_grad_ref[:, rows, :] = jnp.concatenate(other, 1).astype(BF16)


def vmem():
    return pl.BlockSpec(memory_space=pltpu.VMEM)


def tables_in():
    first, last, middle, back, twist = make_tables()
    wide = jnp.broadcast_to(jnp.asarray(twist)[:, :, None], (SLOTS, 2 * STEP, STEP))
    return [jnp.asarray(first), jnp.asarray(last), jnp.asarray(middle), jnp.asarray(back), wide]


def convolved(ext_ref, taps, masks, stream):
    total = taps(0, stream) * ext_ref[stream, pl.ds(8, STEP), :]
    for i in (1, 2):
        total = total + taps(i, stream) * ext_ref[stream, pl.ds(8 - i, STEP), :] * masks[i - 1]
    return total


def fill_extended(rows, early, ext_ref):
    for s in range(3):
        ext_ref[s, pl.ds(6, 2), :] = early(s).astype(F32)[14:]
        ext_ref[s, pl.ds(8, STEP), :] = rows(s).astype(F32)


def rows_spec(lead, rows):
    return pl.BlockSpec((lead, rows, WIDE), lambda i: (0, 0, i))


def flat_spec(rows):
    return pl.BlockSpec((rows, WIDE), lambda i: (0, i))


def chan_spec(rows=STEP):
    return pl.BlockSpec((4, rows, STEP), lambda i: (i, 0, 0))


def slab_spec(rows=STEP):
    return pl.BlockSpec((1, rows, WIDE), lambda i: (i, 0, 0))


def pair_spec(rows=STEP):
    return pl.BlockSpec((1, rows, WIDE), lambda i: (i // 2, 0, i % 2))


def mask_spec():
    return pl.BlockSpec((STEP, 8), lambda i: (0, 0))


def lanes_of(ref):
    return jnp.concatenate([ref[j] for j in range(4)], 1)


def final_kernel(
    streams_ref, early_ref, taps_ref, masks_ref, mix_grad_ref, filtered_ref, prod_grad_ref,
    mix_next_ref, filtered_next_ref, prod_next_ref, head_next_ref,
    grads_ref, tap_ref, ext_ref, conv_ref,
):
    fill_extended(lambda s: streams_ref[s], lambda s: early_ref[s], ext_ref)
    taps = lambda i, s: taps_ref[i, s : s + 1, :]
    behind = [masks_ref[:, i : i + 1] for i in range(2)]
    ahead = [masks_ref[:, 2 + i : 3 + i] for i in range(2)]
    key = convolved(ext_ref, taps, behind, 1)
    value = convolved(ext_ref, taps, behind, 2)
    prod_grad = lanes_of(prod_grad_ref).astype(F32)
    prod_next = lanes_of(prod_next_ref).astype(F32)[:2]
    body = pl.ds(0, STEP)
    tail = pl.ds(STEP, 2)
    query_grad = mix_grad_ref[0].astype(F32) * lanes_of(filtered_ref).astype(F32)
    conv_ref[0, body, :] = query_grad.astype(BF16).astype(F32)
    query_next = mix_next_ref[0].astype(F32) * lanes_of(filtered_next_ref).astype(F32)
    conv_ref[0, tail, :] = query_next.astype(BF16).astype(F32)[:2]
    conv_ref[1, body, :] = prod_grad * value
    conv_ref[1, tail, :] = prod_next * head_next_ref[1, :2, :]
    conv_ref[2, body, :] = prod_grad * key
    conv_ref[2, tail, :] = prod_next * head_next_ref[0, :2, :]
    for s in range(3):
        here = conv_ref[s, body, :]
        grad = taps_ref[0, s : s + 1, :] * here
        sums = [jnp.sum(here * ext_ref[s, pl.ds(8, STEP), :], axis=0, keepdims=True)]
        for i in (1, 2):
            grad = grad + taps_ref[i, s : s + 1, :] * conv_ref[s, pl.ds(i, STEP), :] * ahead[i - 1]
            behind_rows = ext_ref[s, pl.ds(8 - i, STEP), :] * behind[i - 1]
            sums.append(jnp.sum(here * behind_rows, axis=0, keepdims=True))
        grads_ref[s] = grad.astype(BF16)
        for i in range(3):
            for j in range(4):
                tap_ref[j, 3 * i + s : 3 * i + s + 1, :] = sums[i][:, 128 * j : 128 * (j + 1)]
    for j in range(4):
        tap_ref[j, 9:16, :] = jnp.zeros((7, STEP), F32)


def final_grads(streams, early, taps, masks, mix_grad, filtered, prod_grad, nexts):
    return pl.pallas_call(
        final_kernel,
        grid=(8,),
        out_shape=[
            jax.ShapeDtypeStruct((3, STEP, 4096), BF16),
            jax.ShapeDtypeStruct((32, 16, STEP), F32),
        ],
        in_specs=[
            rows_spec(3, STEP), rows_spec(3, 16), rows_spec(3, 3), mask_spec(),
            pair_spec(), chan_spec(), chan_spec(), pair_spec(16), chan_spec(16), chan_spec(16), rows_spec(2, 8),
        ],
        out_specs=[rows_spec(3, STEP), chan_spec(16)],
        scratch_shapes=[pltpu.VMEM((3, STEP + 8, WIDE), F32)] * 2,
        cost_estimate=pl.CostEstimate(flops=3 * 10**7, bytes_accessed=9 * 2**20, transcendentals=0),
        name="final_grads",
    )(streams, early, taps, masks, mix_grad, filtered, prod_grad, *nexts)


class Here:
    def __init__(self):
        self.x, self.w, self.z, self.y, self.c = [lax.axis_index(name) for name in DP + CTX]
        self.ctx = self.z * 8 + self.y * 2 + self.c
        self.dp = self.x * 2 + self.w

    def at_ctx(self, i):
        return (self.x, self.w, i // 8, lax.rem(i // 2, 4), lax.rem(i, 2))

    def at_dp(self, i):
        return (i // 2, lax.rem(i, 2), self.z, self.y, self.c)

    def along_x(self, by):
        return (lax.rem(self.x + by, 4), self.w, self.z, self.y, self.c)

    def along_y(self, by):
        return (self.x, self.w, self.z, lax.rem(self.y + by, 4), self.c)

    def along_z(self, by):
        return (self.x, self.w, lax.rem(self.z + by, 4), self.y, self.c)

    def across_w(self):
        return (self.x, 1 - self.w, self.z, self.y, self.c)

    def across_c(self):
        return (self.x, self.w, self.z, self.y, 1 - self.c)

    def after(self):
        return self.at_ctx(lax.rem(self.ctx + 1, 32))

    def before(self):
        return self.at_ctx(lax.rem(self.ctx + 31, 32))

    def meet(self):
        barrier = pltpu.get_barrier_semaphore()

        @pl.loop(1, 32)
        def _(p):
            place = self.at_ctx(lax.rem(self.ctx + p, 32))
            pl.semaphore_signal(barrier, inc=1, device_id=place, device_id_type=MESH)

        @pl.loop(1, 8)
        def _(p):
            place = self.at_dp(lax.rem(self.dp + p, 8))
            pl.semaphore_signal(barrier, inc=1, device_id=place, device_id_type=MESH)

        pl.semaphore_wait(barrier, 38)


class Links:
    def __init__(self, send, recv, local):
        self.send, self.recv, self.local = send, recv, local

    def to(self, n, place, src, dst):
        return pltpu.make_async_remote_copy(
            src_ref=src, dst_ref=dst, send_sem=self.send.at[n], recv_sem=self.recv.at[n],
            device_id=place, device_id_type=MESH,
        )

    def own(self, n, src, dst):
        return pltpu.make_async_copy(src, dst, self.local.at[n])

    def pairs(self, base, count, me, place, src, dst, same=False, slot=None, source=None):
        def copy(p):
            peer = lax.rem(me + p, count)
            at = dst.at[slot(peer)] if slot else dst.at[me]
            block = source(peer) if source else src if same else src.at[peer]
            return self.to(base + p, place(peer), block, at)

        def start():
            @pl.loop(1, count)
            def _(p):
                copy(p).start()

        def finish():
            @pl.loop(1, count)
            def _(p):
                copy(p).wait()

        return start, finish


def sems(count):
    return [pltpu.SemaphoreType.DMA((count,)), pltpu.SemaphoreType.DMA((count,)), pltpu.SemaphoreType.DMA((16,))]


def anywhere():
    return pl.BlockSpec(memory_space=pl.ANY)


def comm_call(kernel, name, number, count, out_shape, args, in_specs=None, out_specs=None, scratch=(), room=40):
    return pl.pallas_call(
        kernel,
        out_shape=out_shape,
        in_specs=in_specs or [anywhere()] * len(args),
        out_specs=out_specs or [anywhere()] * len(out_shape),
        scratch_shapes=list(scratch) + sems(count),
        compiler_params=pltpu.CompilerParams(
            collective_id=number, has_side_effects=True, vmem_limit_bytes=room * 1024 * 1024
        ),
        cost_estimate=pl.CostEstimate(flops=10**6, bytes_accessed=2**24, transcendentals=0),
        name=name,
    )(*args)


def b16(*shape):
    return jax.ShapeDtypeStruct(shape, BF16)


def ring_steps(links, here, base, block, out):
    x = here.x
    half = block.shape[0] // 2
    right = links.to(base, here.along_x(1), block, out.at[x])
    left = links.to(base + 1, here.along_x(3), block, out.at[x])
    mine = links.own(7, block, out.at[x])
    first = out.at[lax.rem(x + 3, 4), pl.ds(0, half)]
    second = out.at[lax.rem(x + 1, 4), pl.ds(half, half)]
    right_half = links.to(base + 2, here.along_x(1), first, first)
    left_half = links.to(base + 3, here.along_x(3), second, second)

    def begin():
        right.start()
        left.start()
        mine.start()

    def forward():
        right.wait_recv()
        right_half.start()
        left.wait_recv()
        left_half.start()

    def finish():
        right_half.wait()
        left_half.wait()
        right.wait_send()
        left.wait_send()
        mine.wait()

    return begin, forward, finish


def mix_grad_product(own_ref, pair_ref, out_ref, slab, core):
    def step(k, total):
        cols = pl.ds(pl.multiple_of(k * 1024, 1024), 1024)
        left = own_ref[:, :, cols].reshape(512, 1024)
        right = pair_ref[slab, core, :, :, cols].reshape(256, 1024)
        return total + lax.dot_general(left, right, (((1,), (1,)), ((), ())), preferred_element_type=F32)

    total = lax.fori_loop(0, 4, step, jnp.zeros((512, 256), F32))
    cols = pl.ds(pl.multiple_of(slab * 512 + core * 256, 256), 256)
    out_ref[:, :, cols] = total.astype(BF16).reshape(4, STEP, 256)


def wide_cols(i):
    return pl.ds(pl.multiple_of(i * WIDE, WIDE), WIDE)


def first_kernel(
    grad, weight, filt, streams, taps_ref, masks_ref, first_ref, last_ref, mid_ref, back_ref, twist_ref,
    mix_out, filtered_out, early_ref, filter_out,
    head_out, mix_next_out, filtered_next_out, prod_out, prod_next_out, rows_out,
    own_out, spec_prod, spec_filt, flip_out, grads_out, mixed_out, turned_ref,
    pair_ref, prod_ref, filt_ref, yp_ref, yf_ref, mix_ref, filtered_ref, grads_ref, mixed_ref, flip_ref,
    query, head_ref, stage_ref, ext_ref,
    send, recv, local,
):
    here = Here()
    links = Links(send, recv, local)
    x, w, y, c = here.x, here.w, here.y, here.c
    here.meet()
    right = links.to(0, here.along_x(1), grad, own_out.at[x])
    left = links.to(1, here.along_x(3), grad, own_out.at[x])
    share = links.to(2, here.across_w(), weight.at[c, y], pair_ref.at[w, c, y])
    prods = links.pairs(16, 32, here.ctx, here.at_ctx, filtered_ref, prod_ref)
    early = links.to(137, here.after(), streams.at[:, pl.ds(112, 16)], early_ref)
    filts = links.pairs(48, 8, here.dp, here.at_dp, filt, filt_ref, same=True)
    flip = links.to(3, here.across_w(), grad, flip_ref)
    heads = links.to(4, here.before(), head_ref, head_out)
    share.start()
    early.start()
    right.start()
    left.start()
    locals_ = [
        links.own(0, grad, own_out.at[x]),
        links.own(1, weight, pair_ref.at[w]),
        links.own(3, filt, filt_ref.at[here.dp]),
    ]
    for copy in locals_:
        copy.start()
    filts[0]()
    masks = [masks_ref[:, i : i + 1] for i in range(2)]

    def fetch(i):
        slot = lax.rem(i, 2)
        return links.own(8 + slot, streams.at[:, :, wide_cols(i)], stage_ref.at[slot])

    fetch(0).start()
    early.wait_recv()

    @pl.loop(0, 8)
    def _(i):
        @pl.when(i < 7)
        def _():
            fetch(i + 1).start()

        fetch(i).wait()
        slot, cols = lax.rem(i, 2), wide_cols(i)
        fill_extended(lambda s: stage_ref[slot, s], lambda s: early_ref[s, :, cols], ext_ref)
        taps = lambda t, s: taps_ref[t, s : s + 1, cols]
        query[:, cols] = convolved(ext_ref, taps, masks, 0).astype(BF16)
        key = convolved(ext_ref, taps, masks, 1)
        value = convolved(ext_ref, taps, masks, 2)
        head_ref[0, :, cols] = key[:8]
        head_ref[1, :, cols] = value[:8]
        product = (key * value).astype(BF16)
        for j in range(4):
            filtered_ref[4 * i + j] = product[:, 128 * j : 128 * (j + 1)]

    def piece(row, part=None):
        ref = pair_ref.at[1 - w, c, row]
        return ref if part is None else ref.at[pl.ds(32 * part, 32)]

    def pass_on(n, place, row, part=None):
        copy = links.to(n, place, piece(row, part), piece(row, part))
        copy.start()
        return copy

    behind, ahead, far = lax.rem(y + 3, 4), lax.rem(y + 1, 4), lax.rem(y + 2, 4)
    share.wait_recv()
    up = pass_on(5, here.along_y(1), y)
    down = pass_on(6, here.along_y(3), y)
    over = [pass_on(7, here.across_c(), y)]
    prods[0]()
    prod_ref[here.ctx] = filtered_ref[here.ctx]
    heads.start()
    up.wait_recv()
    up_half = pass_on(8, here.along_y(1), behind, 0)
    over.append(pass_on(9, here.across_c(), behind))
    down.wait_recv()
    down_half = pass_on(10, here.along_y(3), ahead, 1)
    over.append(pass_on(11, here.across_c(), ahead))
    right.wait_recv()
    half = own_out.at[lax.rem(x + 3, 4), pl.ds(0, 64)]
    right_half = links.to(12, here.along_x(1), half, half)
    right_half.start()
    left.wait_recv()
    half = own_out.at[lax.rem(x + 1, 4), pl.ds(64, 64)]
    left_half = links.to(13, here.along_x(3), half, half)
    left_half.start()
    up_half.wait_recv()
    down_half.wait_recv()
    over.append(pass_on(14, here.across_c(), far))
    prods[1]()
    filts[1]()
    flip.start()
    for copy in locals_:
        copy.wait()

    filter_forward_kernel(
        prod_ref, filt_ref, first_ref, last_ref, mid_ref, back_ref, twist_ref,
        filtered_ref, spec_prod, spec_filt, yp_ref, yf_ref,
    )
    filtereds = links.pairs(56, 32, here.ctx, here.at_ctx, filtered_ref, filtered_out)
    filtereds[0]()
    filtered_out[here.ctx] = filtered_ref[here.ctx]

    right_half.wait()
    left_half.wait()
    for copy in over:
        copy.wait()

    @pl.loop(0, 4)
    def _(i):
        mix_grad_product(own_out, pair_ref, mix_ref, i // 2, lax.rem(i, 2))

    for copy in (right, left, share, up, down, up_half, down_half, early):
        copy.wait_send()
    mixes = links.pairs(88, 4, x, lambda i: (i, w, here.z, y, c), mix_ref, mix_out)
    mixes[0]()
    mix_out[x] = mix_ref[x]
    flip.wait()
    ring = ring_steps(links, here, 92, flip_ref, flip_out)
    mixes[1]()
    ring[0]()

    @pl.loop(0, 8)
    def _(i):
        mix = mix_out[i // 2, :, wide_cols(lax.rem(i, 2))]
        out = (mix.astype(F32) * query[:, wide_cols(i)].astype(F32)).astype(BF16)
        for j in range(4):
            grads_ref[4 * i + j] = out[:, 128 * j : 128 * (j + 1)]

    grads = links.pairs(96, 32, here.ctx, here.at_ctx, grads_ref, grads_out)
    grads[0]()
    grads_out[here.ctx] = grads_ref[here.ctx]
    mix_next = links.to(15, here.before(), mix_out.at[:, pl.ds(0, 16)], mix_next_out)
    mix_next.start()
    filtereds[1]()

    @pl.loop(0, 8)
    def _(i):
        filtered = jnp.concatenate([filtered_out[4 * i + j] for j in range(4)], 1)
        mixed_ref[i] = (query[:, wide_cols(i)].astype(F32) * filtered.astype(F32)).astype(BF16)

    mixeds = links.pairs(
        128, 8, here.dp, here.at_dp, mixed_ref, mixed_out,
        slot=lambda peer: lax.rem(w + lax.rem(peer, 2), 2) * 4 + x,
    )
    mixeds[0]()
    mixed_out[x] = mixed_ref[here.dp]
    filtered_next = links.to(136, here.before(), filtered_out.at[:, pl.ds(0, 16)], filtered_next_out)
    filtered_next.start()
    ring[1]()
    grads[1]()
    filter_backward_kernel(
        grads_out, spec_prod, spec_filt, first_ref, last_ref, mid_ref, back_ref, twist_ref,
        filtered_ref, grads_ref, yp_ref, yf_ref,
    )
    prod_grads = links.pairs(140, 32, here.ctx, here.at_ctx, filtered_ref, prod_out)
    prod_grads[0]()
    own_grad = links.own(4, filtered_ref.at[here.ctx], prod_out.at[here.ctx])
    own_grad.start()
    mixeds[1]()
    ring[2]()

    @pl.loop(0, 8)
    def _(i):
        at = pl.ds(pl.multiple_of(i * STEP, STEP), STEP)
        turned_ref[:, at] = mixed_out[i].astype(F32).T.astype(BF16)

    @pl.loop(0, 8)
    def _(i):
        cols = wide_cols(i)
        total = dot32(turned_ref[:, :512], own_out[:, :, cols].reshape(512, WIDE))
        total = total + dot32(turned_ref[:, 512:], flip_out[:, :, cols].reshape(512, WIDE))
        total = total.astype(BF16)
        for zz in range(4):
            for yy in range(4):
                for cc in range(2):
                    at = (zz * 8 + yy * 2 + cc) * 16
                    pair_ref[0, cc, yy, 16 * zz : 16 * (zz + 1), cols] = total[at : at + 16]

    half = links.to(138, here.across_c(), pair_ref.at[0, 1 - c], pair_ref.at[1, 0])
    half.start()
    filt_grads = links.pairs(
        172, 8, here.dp, here.at_dp, None, filt_ref, source=lambda peer: grads_ref.at[pl.ds(4 * peer, 4)]
    )
    filt_grads[0]()
    filt_ref[here.dp] = grads_ref[pl.ds(4 * here.dp, 4)]
    half.wait()

    @pl.loop(0, 16)
    def _(i):
        yy = i // 4
        at = pl.ds(pl.multiple_of(lax.rem(i, 4) * 16, 16), 16)
        both = pair_ref[0, c, yy, at, :].astype(F32) + pair_ref[1, 0, yy, at, :].astype(F32)
        pair_ref[1, 1, yy, at, :] = both.astype(BF16)

    rows = links.pairs(180, 4, y, lambda i: (x, w, here.z, i, c), pair_ref.at[1, 1], rows_out)
    rows[0]()
    mine = links.own(2, pair_ref.at[1, 1, y], rows_out.at[y])
    mine.start()
    prod_grads[1]()
    own_grad.wait()
    prod_next = links.to(139, here.before(), prod_out.at[:, pl.ds(0, 16)], prod_next_out)
    prod_next.start()
    filt_grads[1]()
    total = filt_ref[0].astype(F32)
    for i in range(1, 8):
        total = total + filt_ref[i].astype(F32)
    filter_out[...] = total * GRAD_SCALE
    rows[1]()
    for copy in (heads, mix_next, filtered_next, prod_next, mine):
        copy.wait()


def last_kernel(
    parts_ref, rows_ref, total_ref, proj_ref,
    first, second, third, sum_ref, got_ref, send, recv, local,
):
    here = Here()
    links = Links(send, recv, local)
    here.meet()
    scatter = links.pairs(0, 32, here.ctx, here.at_ctx, parts_ref, first)
    share = links.pairs(32, 8, here.dp, here.at_dp, second.at[here.dp], second, same=True)
    gather = links.pairs(40, 32, here.ctx, here.at_ctx, third.at[here.ctx], third, same=True)
    zs = links.pairs(72, 4, here.z, lambda i: (here.x, here.w, i, here.y, here.c), sum_ref, got_ref)
    scatter[0]()
    first[here.ctx] = parts_ref[here.ctx]

    @pl.loop(0, 4)
    def _(z):
        total = rows_ref[0, z].astype(F32)
        for y in range(1, 4):
            total = total + rows_ref[y, z].astype(F32)
        sum_ref[z] = total.astype(BF16)

    zs[0]()
    got_ref[here.z] = sum_ref[here.z]
    scatter[1]()
    second[here.dp] = jnp.sum(first[...], axis=0)
    share[0]()
    share[1]()
    third[here.ctx] = jnp.sum(second[...], axis=0)
    gather[0]()
    zs[1]()
    total = got_ref[0].astype(F32)
    for z in range(1, 4):
        total = total + got_ref[z].astype(F32)
    proj_ref[...] = total * GRAD_SCALE
    gather[1]()
    total_ref[...] = third[...] * GRAD_SCALE


def body(streams, out_grad, proj_weight, long_filter, short_taps, doc_ids):
    rows = streams.shape[1]
    first_row = ((lax.axis_index(DP) * 32) + lax.axis_index(CTX)) * rows
    edge_ids = jnp.full((2,), -1, jnp.int32)
    id_rows = lax.dynamic_slice_in_dim(jnp.concatenate([edge_ids, doc_ids, edge_ids]), first_row, rows + 4)
    own_ids = id_rows[2 : 2 + rows]
    place = lax.axis_index(CTX) * rows + jnp.arange(rows)
    near = [
        jnp.logical_and(id_rows[2 + d : 2 + d + rows] == own_ids, jnp.logical_and(place + d >= 0, place + d < LENGTH))
        for d in (-1, -2, 1, 2)
    ]
    masks = jnp.stack(near + [jnp.zeros((rows,), bool)] * 4, axis=1).astype(F32)
    tables = tables_in()
    blocks = b16(32, STEP, STEP)
    block_room = pltpu.VMEM((32, STEP, STEP), BF16)
    spec_room = pltpu.VMEM((SLOTS, 2 * STEP, STEP), F32)
    group_room = pltpu.VMEM((4, rows, 4096), BF16)
    slab_room = pltpu.VMEM((8, rows, WIDE), BF16)
    (mix_grad, filtered, early, filter_grad, head_next, mix_next, filtered_next, prod_grad, prod_next, row_parts) = comm_call(
        first_kernel, "first", 1, 184,
        [b16(4, rows, 1024), blocks, b16(3, 16, 4096), jax.ShapeDtypeStruct((4, STEP, STEP), F32),
         jax.ShapeDtypeStruct((2, 8, 4096), F32), b16(4, 16, 1024), b16(32, 16, STEP), blocks, b16(32, 16, STEP),
         b16(4, 64, 4096)],
        (out_grad, proj_weight.reshape(2, 4, 64, 4096), long_filter.astype(BF16).reshape(4, STEP, STEP), streams,
         short_taps, masks, *tables),
        in_specs=[anywhere()] * 4 + [vmem()] * 7,
        out_specs=[vmem()] * 4 + [anywhere()] * 6,
        scratch=[
            group_room, spec_room, spec_room, group_room, block_room, slab_room, pltpu.VMEM((WIDE, 1024), BF16),
            pltpu.VMEM((2, 2, 4, 64, 4096), BF16), block_room, pltpu.VMEM((8, 4, STEP, STEP), BF16),
            pltpu.VMEM((64, STEP, STEP), F32), pltpu.VMEM((64, STEP, STEP), F32),
            pltpu.VMEM((4, rows, 1024), BF16), block_room, block_room, slab_room, pltpu.VMEM((rows, 4096), BF16),
            pltpu.VMEM((rows, 4096), BF16), pltpu.VMEM((2, 8, 4096), F32),
            pltpu.VMEM((2, 3, rows, WIDE), BF16), pltpu.VMEM((3, rows + 8, WIDE), F32),
        ],
        room=58,
    )
    stream_grads, tap_parts = final_grads(
        streams, early, short_taps, masks, mix_grad, filtered, prod_grad,
        (mix_next, filtered_next, prod_next, head_next),
    )
    taps, proj_grad = comm_call(
        last_kernel, "last", 5, 76,
        [jax.ShapeDtypeStruct((32, 16, STEP), F32), jax.ShapeDtypeStruct((16, 4096), F32)],
        (tap_parts, row_parts.reshape(4, 4, 16, 4096)),
        in_specs=[vmem(), vmem()], out_specs=[vmem(), vmem()],
        scratch=[
            pltpu.VMEM((32, 16, STEP), F32), pltpu.VMEM((8, 16, STEP), F32), pltpu.VMEM((32, 16, STEP), F32),
            pltpu.VMEM((4, 16, 4096), BF16), pltpu.VMEM((4, 16, 4096), BF16),
        ],
    )
    tap_grad = taps[:, :9, :].transpose(1, 0, 2).reshape(3, 3, 4096)
    return stream_grads, proj_grad, filter_grad.reshape(512, STEP), tap_grad


def solution(mesh):
    devices = np.asarray(mesh.devices).reshape(4, 2, 4, 4, 2)
    fine = Mesh(devices, ("x", "w", "z", "y", "c"))
    every = DP + CTX
    return jax.shard_map(
        body,
        mesh=fine,
        in_specs=(P(None, every, None), P(every, None), P(DP, None), P(DP, CTX), P(), P()),
        out_specs=(P(None, every, None), P(every, None), P(DP, CTX), P()),
        check_vma=False,
    )
```

time: 357 us -> 261 us (0.73)
  Pallas kernels: 305 us -> 250 us
  local copies, waits for them, and re-layouts: 32.2 us -> 7.71 us
  matrix products: 8.7 us -> 0 us
  starting transfers between devices: 4.59 us -> 0 us
    pallas_call x6 -> x0, Pallas kernels: 47.5 us -> none  [the longest x1 11.7 us: filter_forward(): pl.pallas_call(filter_forward_kernel, out_shape=[jax.ShapeDtypeStruct((32...]
    unnamed x71 -> x8, local copies, waits for them, and re-layouts: 23.1 us -> 2.36 us
    dot_general x1 -> x0, matrix products: 8.7 us -> none  [body(): lax.dot_general(own_groups, pair.reshape(1024, 4096), (((1,), (1,)), ((),...]
    pallas_call x5 -> x2, Pallas kernels: 244 us -> 237 us  [comm_call(): pl.pallas_call(kernel, out_shape=out_shape, in_specs=in_specs or [anywher...]
    ppermute x1 -> x0, starting transfers between devices: 4.59 us -> none  [step_along(): lax.ppermute(value, axis, [(i, i + by) for i in range(peers) if 0 <= i +...]
  transfers between devices with their start and end apart: 1 -> 0, of which waited for: 0 -> 0; matrix products, arithmetic and copies ran while one was open for 1% -> 0% of each run, Pallas kernels for 0% -> 0%
where the time goes in v2:
time: 261 us
  Pallas kernels  250 us (96%)
  local copies, waits for them, and re-layouts  7.71 us (3%)
    pallas_call x2, Pallas kernels, comm_call(): pl.pallas_call(kernel, out_shape=out_shape, in_specs=in_specs or [anywher...  237 us
    pallas_call x1, Pallas kernels, final_grads(): pl.pallas_call(final_kernel, grid=(8,), out_shape=[jax.ShapeDtypeStruct((...  13.6 us

profile of v2, /device:TPU:1, one launch (start us, length us, event | category | flops | bytes accessed | tf_op | source)
XLA Modules:
  0.0 260.9 jit_solution(14286275357036893887)
XLA Ops:
  0.6 1.6 convert_element_type.6
  2.3 1.0 concatenate.3
  3.3 0.1 dynamic_slice.3
  3.4 0.1 and_bitcast_fusion
  3.5 0.1 copy.24
  3.6 0.6 convert_element_type.7.masks_ref
  4.3 3.3 %broadcast_in_dim.2.twist_ref = f32[32,256,128]{2,1,0:T(8,128)} broadcast(f32[32,256]{1,0:T(8,128)} %constant.54.clone), dimensions={0,1} | broadcast | bytes 4227072 | tf_op jit(solution)/shard_map/broadcast_in_dim | solution.py:196
  7.5 199.8 %first.1 = (bf16[4,128,1024]{2,1,0:T(8,128)(2,1)}, bf16[32,128,128]{2,1,0:T(8,128)(2,1)}, bf16[3,16,4096]{2,1,0:T(8,128)(2,1)}, f32[4,128,128]{2,1,0:T(8,128)}, ...) custom-call(bf16[128,4096]{1,0:T(8,128)(2,1)} %grad.1, ...), custom_call_target="tpu_custom_call" | custom-call | flops 1000000 | bytes 16777216 | tf_op jit(solution)/shard_map/first/pallas_call | solution.py:390
  207.3 0.0 copy-start
  207.3 13.6 %final_grads.1 = (bf16[3,128,4096]{2,1,0:T(8,128)(2,1)}, f32[32,16,128]{2,1,0:T(8,128)}) custom-call(bf16[3,128,4096]{2,1,0:T(8,128)(2,1)} %streams_ref.1, bf16[3,16,4096]{2,1,0:T(8,128)(2,1)} %get-tuple-element.18.early_ref, f32[3,3,4096]{2,1,0:T(4,128)} %taps_ref.3, f32[128,8]{1,0:T(8,128)} %convert_element_type.7.masks_ref, ...), custom_call_target="tpu_custom_call" | custom-call | flops 30000000 | bytes 9437184 | tf_op jit(solution)/shard_map/final_grads/pallas_call | solution.py:281
  220.9 0.0 copy-done
  220.9 0.0 copy-start.1
  220.9 0.9 copy-done.1
  221.9 0.0 copy-start.2
  221.9 36.8 %last.1 = (f32[32,16,128]{2,1,0:T(8,128)S(1)}, f32[16,4096]{1,0:T(8,128)S(1)}) custom-call(f32[32,16,128]{2,1,0:T(8,128)S(1)} %copy-done.1, bf16[4,4,16,4096]{3,2,1,0:T(8,128)(2,1)S(1)} %bitcast.14), custom_call_target="tpu_custom_call" | custom-call | flops 1000000 | bytes 16777216 | tf_op jit(solution)/shard_map/last/pallas_call | solution.py:390
  258.7 0.1 copy.25
  258.8 0.7 reshape.28
  259.5 0.7 copy.28
  260.2 0.0 copy-done.2
  260.2 0.7 copy.29
  (4 shorter events, 0.1 us)
Async XLA Ops:
  207.3 13.6 %copy-start = (bf16[4,64,4096]{2,1,0:T(8,128)(2,1)S(1)}, bf16[4,64,4096]{2,1,0:T(8,128)(2,1)}, u32[]{:S(2)}) copy-start(bf16[4,64,4096]{2,1,0:T(8,128)(2,1)} %get-tuple-element.28) | copy-start | bytes 6291460
  220.9 1.0 copy-start.1
  221.9 38.4 %copy-start.2 = (f32[4,128,128]{2,1,0:T(8,128)S(1)}, f32[4,128,128]{2,1,0:T(8,128)}, u32[]{:S(2)}) copy-start(f32[4,128,128]{2,1,0:T(8,128)} %get-tuple-element.30) | copy-start | bytes 786436

commit v3 on v2

--- a/solution.py
+++ b/solution.py
@@ -92,7 +92,8 @@
     def _(h):
         rows = pl.ds(pl.multiple_of(16 * h, 16), 16)
         prods = halves_of(prod_ref[:, rows, :].astype(F32))
-        filts = halves_of(filt_ref[:, :, rows, :].reshape(32, 16, STEP).astype(F32))
+        slabs = [filt_ref[i % 2, i // 2, :, rows, :] for i in range(8)]
+        filts = halves_of(jnp.concatenate(slabs, 0).astype(F32))
         for j in range(2):
             wide = dot32(first, jnp.concatenate([prods[j], filts[j]], 1).astype(BF16))
             at = pl.ds(pl.multiple_of(16 * h + 8 * j, 8), 8)
@@ -193,7 +194,7 @@
 
 def tables_in():
     first, last, middle, back, twist = make_tables()
-    wide = jnp.broadcast_to(jnp.asarray(twist)[:, :, None], (SLOTS, 2 * STEP, STEP))
+    wide = jnp.asarray(np.ascontiguousarray(np.broadcast_to(twist[:, :, None], (SLOTS, 2 * STEP, STEP))))
     return [jnp.asarray(first), jnp.asarray(last), jnp.asarray(middle), jnp.asarray(back), wide]
 
 
@@ -210,92 +211,6 @@
         ext_ref[s, pl.ds(8, STEP), :] = rows(s).astype(F32)
 
 
-def rows_spec(lead, rows):
-    return pl.BlockSpec((lead, rows, WIDE), lambda i: (0, 0, i))
-
-
-def flat_spec(rows):
-    return pl.BlockSpec((rows, WIDE), lambda i: (0, i))
-
-
-def chan_spec(rows=STEP):
-    return pl.BlockSpec((4, rows, STEP), lambda i: (i, 0, 0))
-
-
-def slab_spec(rows=STEP):
-    return pl.BlockSpec((1, rows, WIDE), lambda i: (i, 0, 0))
-
-
-def pair_spec(rows=STEP):
-    return pl.BlockSpec((1, rows, WIDE), lambda i: (i // 2, 0, i % 2))
-
-
-def mask_spec():
-    return pl.BlockSpec((STEP, 8), lambda i: (0, 0))
-
-
-def lanes_of(ref):
-    return jnp.concatenate([ref[j] for j in range(4)], 1)
-
-
-def final_kernel(
-    streams_ref, early_ref, taps_ref, masks_ref, mix_grad_ref, filtered_ref, prod_grad_ref,
-    mix_next_ref, filtered_next_ref, prod_next_ref, head_next_ref,
-    grads_ref, tap_ref, ext_ref, conv_ref,
-):
-    fill_extended(lambda s: streams_ref[s], lambda s: early_ref[s], ext_ref)
-    taps = lambda i, s: taps_ref[i, s : s + 1, :]
-    behind = [masks_ref[:, i : i + 1] for i in range(2)]
-    ahead = [masks_ref[:, 2 + i : 3 + i] for i in range(2)]
-    key = convolved(ext_ref, taps, behind, 1)
-    value = convolved(ext_ref, taps, behind, 2)
-    prod_grad = lanes_of(prod_grad_ref).astype(F32)
-    prod_next = lanes_of(prod_next_ref).astype(F32)[:2]
-    body = pl.ds(0, STEP)
-    tail = pl.ds(STEP, 2)
-    query_grad = mix_grad_ref[0].astype(F32) * lanes_of(filtered_ref).astype(F32)
-    conv_ref[0, body, :] = query_grad.astype(BF16).astype(F32)
-    query_next = mix_next_ref[0].astype(F32) * lanes_of(filtered_next_ref).astype(F32)
-    conv_ref[0, tail, :] = query_next.astype(BF16).astype(F32)[:2]
-    conv_ref[1, body, :] = prod_grad * value
-    conv_ref[1, tail, :] = prod_next * head_next_ref[1, :2, :]
-    conv_ref[2, body, :] = prod_grad * key
-    conv_ref[2, tail, :] = prod_next * head_next_ref[0, :2, :]
-    for s in range(3):
-        here = conv_ref[s, body, :]
-        grad = taps_ref[0, s : s + 1, :] * here
-        sums = [jnp.sum(here * ext_ref[s, pl.ds(8, STEP), :], axis=0, keepdims=True)]
-        for i in (1, 2):
-            grad = grad + taps_ref[i, s : s + 1, :] * conv_ref[s, pl.ds(i, STEP), :] * ahead[i - 1]
-            behind_rows = ext_ref[s, pl.ds(8 - i, STEP), :] * behind[i - 1]
-            sums.append(jnp.sum(here * behind_rows, axis=0, keepdims=True))
-        grads_ref[s] = grad.astype(BF16)
-        for i in range(3):
-            for j in range(4):
-                tap_ref[j, 3 * i + s : 3 * i + s + 1, :] = sums[i][:, 128 * j : 128 * (j + 1)]
-    for j in range(4):
-        tap_ref[j, 9:16, :] = jnp.zeros((7, STEP), F32)
-
-
-def final_grads(streams, early, taps, masks, mix_grad, filtered, prod_grad, nexts):
-    return pl.pallas_call(
-        final_kernel,
-        grid=(8,),
-        out_shape=[
-            jax.ShapeDtypeStruct((3, STEP, 4096), BF16),
-            jax.ShapeDtypeStruct((32, 16, STEP), F32),
-        ],
-        in_specs=[
-            rows_spec(3, STEP), rows_spec(3, 16), rows_spec(3, 3), mask_spec(),
-            pair_spec(), chan_spec(), chan_spec(), pair_spec(16), chan_spec(16), chan_spec(16), rows_spec(2, 8),
-        ],
-        out_specs=[rows_spec(3, STEP), chan_spec(16)],
-        scratch_shapes=[pltpu.VMEM((3, STEP + 8, WIDE), F32)] * 2,
-        cost_estimate=pl.CostEstimate(flops=3 * 10**7, bytes_accessed=9 * 2**20, transcendentals=0),
-        name="final_grads",
-    )(streams, early, taps, masks, mix_grad, filtered, prod_grad, *nexts)
-
-
 class Here:
     def __init__(self):
         self.x, self.w, self.z, self.y, self.c = [lax.axis_index(name) for name in DP + CTX]
@@ -352,6 +267,12 @@
     def to(self, n, place, src, dst):
         return pltpu.make_async_remote_copy(
             src_ref=src, dst_ref=dst, send_sem=self.send.at[n], recv_sem=self.recv.at[n],
+            device_id=place, device_id_type=MESH,
+        )
+
+    def apart(self, sent, got, place, src, dst):
+        return pltpu.make_async_remote_copy(
+            src_ref=src, dst_ref=dst, send_sem=self.send.at[sent], recv_sem=self.recv.at[got],
             device_id=place, device_id_type=MESH,
         )
 
@@ -405,12 +326,12 @@
     return jax.ShapeDtypeStruct(shape, BF16)
 
 
-def ring_steps(links, here, base, block, out):
+def ring_steps(links, here, base, block, out, placed=False, local=7):
     x = here.x
     half = block.shape[0] // 2
     right = links.to(base, here.along_x(1), block, out.at[x])
     left = links.to(base + 1, here.along_x(3), block, out.at[x])
-    mine = links.own(7, block, out.at[x])
+    mine = None if placed else links.own(local, block, out.at[x])
     first = out.at[lax.rem(x + 3, 4), pl.ds(0, half)]
     second = out.at[lax.rem(x + 1, 4), pl.ds(half, half)]
     right_half = links.to(base + 2, here.along_x(1), first, first)
@@ -419,7 +340,8 @@
     def begin():
         right.start()
         left.start()
-        mine.start()
+        if mine is not None:
+            mine.start()
 
     def forward():
         right.wait_recv()
@@ -432,21 +354,19 @@
         left_half.wait()
         right.wait_send()
         left.wait_send()
-        mine.wait()
+        if mine is not None:
+            mine.wait()
 
     return begin, forward, finish
 
 
 def mix_grad_product(own_ref, pair_ref, out_ref, slab, core):
-    def step(k, total):
-        cols = pl.ds(pl.multiple_of(k * 1024, 1024), 1024)
-        left = own_ref[:, :, cols].reshape(512, 1024)
-        right = pair_ref[slab, core, :, :, cols].reshape(256, 1024)
-        return total + lax.dot_general(left, right, (((1,), (1,)), ((), ())), preferred_element_type=F32)
-
-    total = lax.fori_loop(0, 4, step, jnp.zeros((512, 256), F32))
+    right = pair_ref[slab, core].reshape(256, 4096)
     cols = pl.ds(pl.multiple_of(slab * 512 + core * 256, 256), 256)
-    out_ref[:, :, cols] = total.astype(BF16).reshape(4, STEP, 256)
+    for part in range(2):
+        left = own_ref[2 * part : 2 * part + 2].reshape(256, 4096)
+        total = lax.dot_general(left, right, (((1,), (1,)), ((), ())), preferred_element_type=F32)
+        out_ref[2 * part : 2 * part + 2, :, cols] = total.astype(BF16).reshape(2, STEP, 256)
 
 
 def wide_cols(i):
@@ -454,38 +374,52 @@
 
 
 def first_kernel(
-    grad, weight, filt, streams, taps_ref, masks_ref, first_ref, last_ref, mid_ref, back_ref, twist_ref,
-    mix_out, filtered_out, early_ref, filter_out,
-    head_out, mix_next_out, filtered_next_out, prod_out, prod_next_out, rows_out,
+    grad, weight, filt, streams, taps_ref, masks_ref, first_in, last_in, mid_in, back_in, twist_in,
+    stream_out, proj_out, filter_out, tap_out,
+    mix_out, filtered_out, early_ref, head_out, mix_next_out, filtered_next_out, prod_next_out, rows_ref, step_ref,
+    result_ref, conv_ref, taps_part, tap_first, tap_second, tap_third, row_sum, row_got,
+    filt_b, first_ref, last_ref, mid_ref, back_ref, twist_ref,
     own_out, spec_prod, spec_filt, flip_out, grads_out, mixed_out, turned_ref,
-    pair_ref, prod_ref, filt_ref, yp_ref, yf_ref, mix_ref, filtered_ref, grads_ref, mixed_ref, flip_ref,
+    pair_ref, prod_ref, filt_ref, yp_ref, yf_ref, mix_ref, filtered_ref, grads_ref,
     query, head_ref, stage_ref, ext_ref,
     send, recv, local,
 ):
     here = Here()
     links = Links(send, recv, local)
     x, w, y, c = here.x, here.w, here.y, here.c
+    tables = [
+        links.own(n, src, dst)
+        for n, src, dst in (
+            (4, first_in, first_ref), (5, mid_in, mid_ref), (6, twist_in, twist_ref), (12, back_in, back_ref),
+            (13, last_in, last_ref),
+        )
+    ]
+    for copy in tables:
+        copy.start()
+    filt_b[...] = filt[...].astype(BF16)
     here.meet()
     right = links.to(0, here.along_x(1), grad, own_out.at[x])
     left = links.to(1, here.along_x(3), grad, own_out.at[x])
     share = links.to(2, here.across_w(), weight.at[c, y], pair_ref.at[w, c, y])
     prods = links.pairs(16, 32, here.ctx, here.at_ctx, filtered_ref, prod_ref)
     early = links.to(137, here.after(), streams.at[:, pl.ds(112, 16)], early_ref)
-    filts = links.pairs(48, 8, here.dp, here.at_dp, filt, filt_ref, same=True)
-    flip = links.to(3, here.across_w(), grad, flip_ref)
+    filt_share = links.to(48, here.across_w(), filt_b, filt_ref.at[w, x])
+    filt_own = ring_steps(links, here, 184, filt_b, filt_ref.at[w], local=3)
+    filt_other = ring_steps(links, here, 188, filt_ref.at[1 - w, x], filt_ref.at[1 - w], placed=True)
+    flip = links.to(3, here.across_w(), grad, flip_out.at[x])
     heads = links.to(4, here.before(), head_ref, head_out)
+    early.start()
+    filt_share.start()
+    filt_own[0]()
     share.start()
-    early.start()
     right.start()
     left.start()
     locals_ = [
         links.own(0, grad, own_out.at[x]),
         links.own(1, weight, pair_ref.at[w]),
-        links.own(3, filt, filt_ref.at[here.dp]),
     ]
     for copy in locals_:
         copy.start()
-    filts[0]()
     masks = [masks_ref[:, i : i + 1] for i in range(2)]
 
     def fetch(i):
@@ -494,6 +428,9 @@
 
     fetch(0).start()
     early.wait_recv()
+    filt_share.wait()
+    filt_other[0]()
+    filt_own[1]()
 
     @pl.loop(0, 8)
     def _(i):
@@ -513,6 +450,8 @@
         product = (key * value).astype(BF16)
         for j in range(4):
             filtered_ref[4 * i + j] = product[:, 128 * j : 128 * (j + 1)]
+
+    filt_other[1]()
 
     def piece(row, part=None):
         ref = pair_ref.at[1 - w, c, row]
@@ -545,15 +484,32 @@
     half = own_out.at[lax.rem(x + 1, 4), pl.ds(64, 64)]
     left_half = links.to(13, here.along_x(3), half, half)
     left_half.start()
+    flip.start()
     up_half.wait_recv()
     down_half.wait_recv()
     over.append(pass_on(14, here.across_c(), far))
+    filt_own[2]()
+    filt_other[2]()
     prods[1]()
-    filts[1]()
-    flip.start()
     for copy in locals_:
         copy.wait()
 
+    right_half.wait()
+    left_half.wait()
+    for copy in over:
+        copy.wait()
+
+    @pl.loop(0, 4)
+    def _(i):
+        mix_grad_product(own_out, pair_ref, mix_ref, i // 2, lax.rem(i, 2))
+
+    for copy in (right, left, share, up, down, up_half, down_half, early):
+        copy.wait_send()
+    mixes = links.pairs(88, 4, x, lambda i: (i, w, here.z, y, c), mix_ref, mix_out)
+    mixes[0]()
+    mix_out[x] = mix_ref[x]
+    for copy in tables:
+        copy.wait()
     filter_forward_kernel(
         prod_ref, filt_ref, first_ref, last_ref, mid_ref, back_ref, twist_ref,
         filtered_ref, spec_prod, spec_filt, yp_ref, yf_ref,
@@ -562,22 +518,8 @@
     filtereds[0]()
     filtered_out[here.ctx] = filtered_ref[here.ctx]
 
-    right_half.wait()
-    left_half.wait()
-    for copy in over:
-        copy.wait()
-
-    @pl.loop(0, 4)
-    def _(i):
-        mix_grad_product(own_out, pair_ref, mix_ref, i // 2, lax.rem(i, 2))
-
-    for copy in (right, left, share, up, down, up_half, down_half, early):
-        copy.wait_send()
-    mixes = links.pairs(88, 4, x, lambda i: (i, w, here.z, y, c), mix_ref, mix_out)
-    mixes[0]()
-    mix_out[x] = mix_ref[x]
     flip.wait()
-    ring = ring_steps(links, here, 92, flip_ref, flip_out)
+    ring = ring_steps(links, here, 92, flip_out.at[x], flip_out, placed=True)
     mixes[1]()
     ring[0]()
 
@@ -598,14 +540,16 @@
     @pl.loop(0, 8)
     def _(i):
         filtered = jnp.concatenate([filtered_out[4 * i + j] for j in range(4)], 1)
-        mixed_ref[i] = (query[:, wide_cols(i)].astype(F32) * filtered.astype(F32)).astype(BF16)
+        mixed = (query[:, wide_cols(i)].astype(F32) * filtered.astype(F32)).astype(BF16)
+        mix_ref[i // 2, :, wide_cols(lax.rem(i, 2))] = mixed
 
     mixeds = links.pairs(
-        128, 8, here.dp, here.at_dp, mixed_ref, mixed_out,
+        128, 8, here.dp, here.at_dp, None, mixed_out,
+        source=lambda peer: mix_ref.at[peer // 2, :, wide_cols(lax.rem(peer, 2))],
         slot=lambda peer: lax.rem(w + lax.rem(peer, 2), 2) * 4 + x,
     )
     mixeds[0]()
-    mixed_out[x] = mixed_ref[here.dp]
+    mixed_out[x] = mix_ref[x, :, wide_cols(w)]
     filtered_next = links.to(136, here.before(), filtered_out.at[:, pl.ds(0, 16)], filtered_next_out)
     filtered_next.start()
     ring[1]()
@@ -614,10 +558,9 @@
         grads_out, spec_prod, spec_filt, first_ref, last_ref, mid_ref, back_ref, twist_ref,
         filtered_ref, grads_ref, yp_ref, yf_ref,
     )
-    prod_grads = links.pairs(140, 32, here.ctx, here.at_ctx, filtered_ref, prod_out)
+    prod_grads = links.pairs(140, 32, here.ctx, here.at_ctx, filtered_ref, prod_ref)
     prod_grads[0]()
-    own_grad = links.own(4, filtered_ref.at[here.ctx], prod_out.at[here.ctx])
-    own_grad.start()
+    prod_ref[here.ctx] = filtered_ref[here.ctx]
     mixeds[1]()
     ring[2]()
 
@@ -641,10 +584,11 @@
     half = links.to(138, here.across_c(), pair_ref.at[0, 1 - c], pair_ref.at[1, 0])
     half.start()
     filt_grads = links.pairs(
-        172, 8, here.dp, here.at_dp, None, filt_ref, source=lambda peer: grads_ref.at[pl.ds(4 * peer, 4)]
+        172, 8, here.dp, here.at_dp, None, filt_ref, slot=lambda peer: (w, x),
+        source=lambda peer: grads_ref.at[pl.ds(4 * peer, 4)]
     )
     filt_grads[0]()
-    filt_ref[here.dp] = grads_ref[pl.ds(4 * here.dp, 4)]
+    filt_ref[w, x] = grads_ref[pl.ds(4 * here.dp, 4)]
     half.wait()
 
     @pl.loop(0, 16)
@@ -654,60 +598,141 @@
         both = pair_ref[0, c, yy, at, :].astype(F32) + pair_ref[1, 0, yy, at, :].astype(F32)
         pair_ref[1, 1, yy, at, :] = both.astype(BF16)
 
-    rows = links.pairs(180, 4, y, lambda i: (x, w, here.z, i, c), pair_ref.at[1, 1], rows_out)
-    rows[0]()
-    mine = links.own(2, pair_ref.at[1, 1, y], rows_out.at[y])
-    mine.start()
+    up_place, down_place = here.along_y(1), here.along_y(3)
+    y_up, y_down, y_far = lax.rem(y + 1, 4), lax.rem(y + 3, 4), lax.rem(y + 2, 4)
+    far_steps = [
+        links.to(180, up_place, pair_ref.at[1, 1, y_far, pl.ds(0, 32)], step_ref.at[0]),
+        links.to(181, down_place, pair_ref.at[1, 1, y_far, pl.ds(32, 32)], step_ref.at[1]),
+    ]
+    for copy in far_steps:
+        copy.start()
+    for copy in far_steps:
+        copy.wait()
+    for side, row in ((0, y_up), (1, y_down)):
+        for part in range(2):
+            at = pl.ds(32 * side + 16 * part, 16)
+            both = pair_ref[1, 1, row, at, :].astype(F32)
+            both = both + step_ref[side, 16 * part : 16 * (part + 1), :].astype(F32)
+            pair_ref[1, 1, row, at, :] = both.astype(BF16)
+    near_steps = [
+        links.to(182, up_place, pair_ref.at[1, 1, y_up], rows_ref.at[0]),
+        links.to(183, down_place, pair_ref.at[1, 1, y_down], rows_ref.at[1]),
+    ]
+    for copy in near_steps:
+        copy.start()
     prod_grads[1]()
-    own_grad.wait()
-    prod_next = links.to(139, here.before(), prod_out.at[:, pl.ds(0, 16)], prod_next_out)
+    prod_next = links.to(139, here.before(), prod_ref.at[:, pl.ds(0, 16)], prod_next_out)
     prod_next.start()
     filt_grads[1]()
-    total = filt_ref[0].astype(F32)
+    total = filt_ref[0, 0].astype(F32)
     for i in range(1, 8):
-        total = total + filt_ref[i].astype(F32)
+        total = total + filt_ref[i % 2, i // 2].astype(F32)
     filter_out[...] = total * GRAD_SCALE
-    rows[1]()
-    for copy in (heads, mix_next, filtered_next, prod_next, mine):
+    for copy in (heads, mix_next, filtered_next, prod_next):
         copy.wait()
-
-
-def last_kernel(
-    parts_ref, rows_ref, total_ref, proj_ref,
-    first, second, third, sum_ref, got_ref, send, recv, local,
-):
-    here = Here()
-    links = Links(send, recv, local)
-    here.meet()
-    scatter = links.pairs(0, 32, here.ctx, here.at_ctx, parts_ref, first)
-    share = links.pairs(32, 8, here.dp, here.at_dp, second.at[here.dp], second, same=True)
-    gather = links.pairs(40, 32, here.ctx, here.at_ctx, third.at[here.ctx], third, same=True)
-    zs = links.pairs(72, 4, here.z, lambda i: (here.x, here.w, i, here.y, here.c), sum_ref, got_ref)
-    scatter[0]()
-    first[here.ctx] = parts_ref[here.ctx]
+    ahead = [masks_ref[:, 2 + i : 3 + i] for i in range(2)]
+
+    def store(i):
+        slot = lax.rem(i, 2)
+        return links.own(10 + slot, result_ref.at[slot], stream_out.at[:, :, wide_cols(i)])
+
+    fetch(0).start()
+
+    @pl.loop(0, 8)
+    def _(i):
+        @pl.when(i < 7)
+        def _():
+            fetch(i + 1).start()
+
+        @pl.when(i >= 2)
+        def _():
+            store(i - 2).wait()
+
+        fetch(i).wait()
+        slot, cols = lax.rem(i, 2), wide_cols(i)
+        mix_cols = wide_cols(lax.rem(i, 2))
+        fill_extended(lambda s: stage_ref[slot, s], lambda s: early_ref[s, :, cols], ext_ref)
+        taps = lambda t, s: taps_ref[t, s : s + 1, cols]
+        key = convolved(ext_ref, taps, masks, 1)
+        value = convolved(ext_ref, taps, masks, 2)
+
+        def lanes(ref):
+            return jnp.concatenate([ref[4 * i + j] for j in range(4)], 1).astype(F32)
+
+        product_grad = lanes(prod_ref)
+        product_next = lanes(prod_next_out)[:2]
+        inner, outer = pl.ds(0, STEP), pl.ds(STEP, 2)
+        query_grad = mix_out[i // 2, :, mix_cols].astype(F32) * lanes(filtered_out)
+        conv_ref[0, inner, :] = query_grad.astype(BF16).astype(F32)
+        query_next = mix_next_out[i // 2, :, mix_cols].astype(F32) * lanes(filtered_next_out)
+        conv_ref[0, outer, :] = query_next.astype(BF16).astype(F32)[:2]
+        conv_ref[1, inner, :] = product_grad * value
+        conv_ref[1, outer, :] = product_next * head_out[1, :2, cols]
+        conv_ref[2, inner, :] = product_grad * key
+        conv_ref[2, outer, :] = product_next * head_out[0, :2, cols]
+        for s in range(3):
+            at_here = conv_ref[s, inner, :]
+            grad_rows = taps(0, s) * at_here
+            sums = [jnp.sum(at_here * ext_ref[s, pl.ds(8, STEP), :], axis=0, keepdims=True)]
+            for t in (1, 2):
+                grad_rows = grad_rows + taps(t, s) * conv_ref[s, pl.ds(t, STEP), :] * ahead[t - 1]
+                behind_rows = ext_ref[s, pl.ds(8 - t, STEP), :] * masks[t - 1]
+                sums.append(jnp.sum(at_here * behind_rows, axis=0, keepdims=True))
+            result_ref[slot, s] = grad_rows.astype(BF16)
+            for t in range(3):
+                for j in range(4):
+                    taps_part[4 * i + j, 3 * t + s : 3 * t + s + 1, :] = sums[t][:, 128 * j : 128 * (j + 1)]
+        for j in range(4):
+            taps_part[4 * i + j, 9:16, :] = jnp.zeros((7, STEP), F32)
+        store(i).start()
+        for j in range(4):
+            peer = 4 * i + j
+
+            @pl.when(peer != here.ctx)
+            def _():
+                links.apart(
+                    192 + peer, 192 + here.ctx, here.at_ctx(peer), taps_part.at[peer], tap_first.at[here.ctx]
+                ).start()
+
+    spread = links.pairs(224, 8, here.dp, here.at_dp, tap_second.at[here.dp], tap_second, same=True)
+    gather = links.pairs(232, 32, here.ctx, here.at_ctx, tap_third.at[here.ctx], tap_third, same=True)
+    zs = links.pairs(264, 4, here.z, lambda i: (x, w, i, y, c), row_sum, row_got)
+    tap_first[here.ctx] = taps_part[here.ctx]
+    for copy in near_steps:
+        copy.wait()
 
     @pl.loop(0, 4)
-    def _(z):
-        total = rows_ref[0, z].astype(F32)
-        for y in range(1, 4):
-            total = total + rows_ref[y, z].astype(F32)
-        sum_ref[z] = total.astype(BF16)
+    def _(i):
+        at = pl.ds(pl.multiple_of(i * 16, 16), 16)
+        total = pair_ref[1, 1, y, at, :].astype(F32)
+        for k in range(2):
+            total = total + rows_ref[k, at, :].astype(F32)
+        row_sum[i] = total.astype(BF16)
 
     zs[0]()
-    got_ref[here.z] = sum_ref[here.z]
-    scatter[1]()
-    second[here.dp] = jnp.sum(first[...], axis=0)
-    share[0]()
-    share[1]()
-    third[here.ctx] = jnp.sum(second[...], axis=0)
+    row_got[here.z] = row_sum[here.z]
+
+    @pl.loop(1, 32)
+    def _(p):
+        peer = lax.rem(here.ctx + p, 32)
+        links.apart(192 + peer, 192 + peer, here.at_ctx(peer), taps_part.at[peer], tap_first.at[peer]).wait()
+
+    tap_second[here.dp] = jnp.sum(tap_first[...], axis=0)
+    spread[0]()
+    spread[1]()
+    tap_third[here.ctx] = jnp.sum(tap_second[...], axis=0)
     gather[0]()
     zs[1]()
-    total = got_ref[0].astype(F32)
-    for z in range(1, 4):
-        total = total + got_ref[z].astype(F32)
-    proj_ref[...] = total * GRAD_SCALE
+    total = row_got[0].astype(F32)
+    for i in range(1, 4):
+        total = total + row_got[i].astype(F32)
+    proj_out[...] = total * GRAD_SCALE
+    store(6).wait()
+    store(7).wait()
     gather[1]()
-    total_ref[...] = third[...] * GRAD_SCALE
+    totals = jnp.concatenate([tap_third[j] for j in range(32)], 1) * GRAD_SCALE
+    for t in range(3):
+        tap_out[t] = totals[3 * t : 3 * t + 3]
 
 
 def body(streams, out_grad, proj_weight, long_filter, short_taps, doc_ids):
@@ -723,46 +748,39 @@
     ]
     masks = jnp.stack(near + [jnp.zeros((rows,), bool)] * 4, axis=1).astype(F32)
     tables = tables_in()
-    blocks = b16(32, STEP, STEP)
     block_room = pltpu.VMEM((32, STEP, STEP), BF16)
     spec_room = pltpu.VMEM((SLOTS, 2 * STEP, STEP), F32)
     group_room = pltpu.VMEM((4, rows, 4096), BF16)
     slab_room = pltpu.VMEM((8, rows, WIDE), BF16)
-    (mix_grad, filtered, early, filter_grad, head_next, mix_next, filtered_next, prod_grad, prod_next, row_parts) = comm_call(
-        first_kernel, "first", 1, 184,
-        [b16(4, rows, 1024), blocks, b16(3, 16, 4096), jax.ShapeDtypeStruct((4, STEP, STEP), F32),
-         jax.ShapeDtypeStruct((2, 8, 4096), F32), b16(4, 16, 1024), b16(32, 16, STEP), blocks, b16(32, 16, STEP),
-         b16(4, 64, 4096)],
-        (out_grad, proj_weight.reshape(2, 4, 64, 4096), long_filter.astype(BF16).reshape(4, STEP, STEP), streams,
+    half_blocks = pltpu.VMEM((32, 16, STEP), BF16)
+    part_room = pltpu.VMEM((32, 16, STEP), F32)
+    head_room = pltpu.VMEM((2, 8, 4096), F32)
+    stage_room = pltpu.VMEM((2, 3, rows, WIDE), BF16)
+    ext_room = pltpu.VMEM((3, rows + 8, WIDE), F32)
+    mix_room = pltpu.VMEM((4, rows, 1024), BF16)
+    row_room = pltpu.VMEM((4, 16, 4096), BF16)
+    stream_grads, proj_grad, filter_grad, taps = comm_call(
+        first_kernel, "hyena_backward", 1, 268,
+        [b16(3, rows, 4096), jax.ShapeDtypeStruct((16, 4096), F32), jax.ShapeDtypeStruct((4, STEP, STEP), F32),
+         jax.ShapeDtypeStruct((3, 3, 4096), F32)],
+        (out_grad, proj_weight.reshape(2, 4, 64, 4096), long_filter.reshape(4, STEP, STEP), streams,
          short_taps, masks, *tables),
-        in_specs=[anywhere()] * 4 + [vmem()] * 7,
-        out_specs=[vmem()] * 4 + [anywhere()] * 6,
+        in_specs=[anywhere()] * 2 + [vmem(), anywhere(), vmem(), vmem()] + [anywhere()] * 5,
+        out_specs=[anywhere()] + [vmem()] * 3,
         scratch=[
+            mix_room, block_room, pltpu.VMEM((3, 16, 4096), BF16), head_room, pltpu.VMEM((4, 16, 1024), BF16),
+            half_blocks, half_blocks, pltpu.VMEM((2, 64, 4096), BF16), pltpu.VMEM((2, 32, 4096), BF16),
+            stage_room, ext_room,
+            part_room, part_room, pltpu.VMEM((8, 16, STEP), F32), part_room, row_room, row_room,
+            pltpu.VMEM((4, STEP, STEP), BF16), *[pltpu.VMEM(table.shape, table.dtype) for table in tables],
             group_room, spec_room, spec_room, group_room, block_room, slab_room, pltpu.VMEM((WIDE, 1024), BF16),
-            pltpu.VMEM((2, 2, 4, 64, 4096), BF16), block_room, pltpu.VMEM((8, 4, STEP, STEP), BF16),
+            pltpu.VMEM((2, 2, 4, 64, 4096), BF16), block_room, pltpu.VMEM((2, 4, 4, STEP, STEP), BF16),
             pltpu.VMEM((64, STEP, STEP), F32), pltpu.VMEM((64, STEP, STEP), F32),
-            pltpu.VMEM((4, rows, 1024), BF16), block_room, block_room, slab_room, pltpu.VMEM((rows, 4096), BF16),
-            pltpu.VMEM((rows, 4096), BF16), pltpu.VMEM((2, 8, 4096), F32),
-            pltpu.VMEM((2, 3, rows, WIDE), BF16), pltpu.VMEM((3, rows + 8, WIDE), F32),
+            mix_room, block_room, block_room, pltpu.VMEM((rows, 4096), BF16), head_room, stage_room, ext_room,
         ],
-        room=58,
+        room=62,
     )
-    stream_grads, tap_parts = final_grads(
-        streams, early, short_taps, masks, mix_grad, filtered, prod_grad,
-        (mix_next, filtered_next, prod_next, head_next),
-    )
-    taps, proj_grad = comm_call(
-        last_kernel, "last", 5, 76,
-        [jax.ShapeDtypeStruct((32, 16, STEP), F32), jax.ShapeDtypeStruct((16, 4096), F32)],
-        (tap_parts, row_parts.reshape(4, 4, 16, 4096)),
-        in_specs=[vmem(), vmem()], out_specs=[vmem(), vmem()],
-        scratch=[
-            pltpu.VMEM((32, 16, STEP), F32), pltpu.VMEM((8, 16, STEP), F32), pltpu.VMEM((32, 16, STEP), F32),
-            pltpu.VMEM((4, 16, 4096), BF16), pltpu.VMEM((4, 16, 4096), BF16),
-        ],
-    )
-    tap_grad = taps[:, :9, :].transpose(1, 0, 2).reshape(3, 3, 4096)
-    return stream_grads, proj_grad, filter_grad.reshape(512, STEP), tap_grad
+    return stream_grads, proj_grad, filter_grad.reshape(512, STEP), taps
 
 
 def solution(mesh):

time: 261 us -> 247 us (0.946)
  Pallas kernels: 250 us -> 238 us
    pallas_call x1 -> x0, Pallas kernels: 13.6 us -> none  [final_grads(): pl.pallas_call(final_kernel, grid=(8,), out_shape=[jax.ShapeDtypeStruct((...]
    unnamed x8 -> x10, local copies, waits for them, and re-layouts: 2.36 us -> 6.07 us
    broadcast_in_dim x1 -> x0, local copies, waits for them, and re-layouts: 3.27 us -> none  [tables_in(): jnp.broadcast_to(jnp.asarray(twist)[:, :, None], (SLOTS, 2 * STEP, STEP))]
    pallas_call x2 -> x1, Pallas kernels: 237 us -> 238 us  [comm_call(): pl.pallas_call(kernel, out_shape=out_shape, in_specs=in_specs or [anywher...]
where the time goes in v3:
time: 247 us; the launch traced here: 246 us
  Pallas kernels  238 us (96%)
  local copies, waits for them, and re-layouts  7.95 us (3%)
    pallas_call x1, Pallas kernels, comm_call(): pl.pallas_call(kernel, out_shape=out_shape, in_specs=in_specs or [anywher...  238 us
    unnamed x10, local copies, waits for them, and re-layouts  6.07 us

profile of v3, /device:TPU:1, one launch (start us, length us, event | category | flops | bytes accessed | tf_op | source)
XLA Modules:
  0.0 246.2 jit_solution(2087579438195416351)
XLA Ops:
  0.7 1.0 concatenate.3
  1.7 0.1 dynamic_slice.3
  1.8 0.1 and_bitcast_fusion
  1.9 0.7 copy.20.masks_ref
  2.6 237.5 %hyena_backward.1 = (bf16[3,128,4096]{2,1,0:T(8,128)(2,1)}, f32[16,4096]{1,0:T(8,128)}, f32[4,128,128]{2,1,0:T(8,128)}, f32[3,3,4096]{2,1,0:T(4,128)}) custom-call(bf16[128,4096]{1,0:T(8,128)(2,1)} %grad.1, bf16[2,4,64,4096]{3,2,1,0:T(8,128)(2,1)} %bitcast.11, f32[4,128,128]{2,1,0:T(8,128)} %bitcast.12, bf16[3,128,4096]{2,1,0:T(8,128)(2,1)} %streams.1, ...), custom_call_target="tpu_custom_call" | custom-call | flops 1000000 | bytes 16777216 | tf_op jit(solution)/shard_map/hyena_backward/pallas_call | solution.py:311
  240.2 0.0 copy-start.1
  240.2 0.0 copy-start
  240.2 0.0 copy-start.2
  240.2 4.0 %copy.25 = bf16[3,128,4096]{2,1,0:T(8,128)(2,1)} copy(bf16[3,128,4096]{2,1,0:T(8,128)(2,1)} %get-tuple-element.20) | data formatting | bytes 6291456
  244.2 0.0 copy-done.1
  244.2 0.7 copy.26
  244.9 0.0 copy-done
  244.9 0.7 copy.27
  245.6 0.0 copy-done.2
  245.6 0.7 copy.28
  (4 shorter events, 0.0 us)
Async XLA Ops:
  240.2 4.0 %copy-start.1 = (f32[16,4096]{1,0:T(8,128)S(1)}, f32[16,4096]{1,0:T(8,128)}, u32[]{:S(2)}) copy-start(f32[16,4096]{1,0:T(8,128)} %get-tuple-element.21) | copy-start | bytes 786436
  240.2 4.7 %copy-start = (f32[4,128,128]{2,1,0:T(8,128)S(1)}, f32[4,128,128]{2,1,0:T(8,128)}, u32[]{:S(2)}) copy-start(f32[4,128,128]{2,1,0:T(8,128)} %get-tuple-element.10) | copy-start | bytes 786436
  240.2 5.4 %copy-start.2 = (f32[3,3,4096]{2,1,0:T(4,128)S(1)}, f32[3,3,4096]{2,1,0:T(4,128)}, u32[]{:S(2)}) copy-start(f32[3,3,4096]{2,1,0:T(4,128)} %get-tuple-element.23) | copy-start | bytes 442372

commit v4 on v3

--- a/solution.py
+++ b/solution.py
@@ -484,13 +484,13 @@
     half = own_out.at[lax.rem(x + 1, 4), pl.ds(64, 64)]
     left_half = links.to(13, here.along_x(3), half, half)
     left_half.start()
-    flip.start()
     up_half.wait_recv()
     down_half.wait_recv()
     over.append(pass_on(14, here.across_c(), far))
     filt_own[2]()
     filt_other[2]()
     prods[1]()
+    flip.start()
     for copy in locals_:
         copy.wait()
 

time: 247 us -> 251 us (1.016)
  Pallas kernels: 238 us -> 241 us
    pallas_call x1, Pallas kernels: 238 us -> 241 us  [comm_call(): pl.pallas_call(kernel, out_shape=out_shape, in_specs=in_specs or [anywher...]
where the time goes in v4:
time: 251 us; the launch traced here: 250 us
  Pallas kernels  241 us (96%)
  local copies, waits for them, and re-layouts  7.95 us (3%)
    pallas_call x1, Pallas kernels, comm_call(): pl.pallas_call(kernel, out_shape=out_shape, in_specs=in_specs or [anywher...  241 us
    unnamed x10, local copies, waits for them, and re-layouts  6.07 us

profile of v4, /device:TPU:1, one launch (start us, length us, event | category | flops | bytes accessed | tf_op | source)
XLA Modules:
  0.0 249.8 jit_solution(626964123399565354)
XLA Ops:
  0.7 1.0 concatenate.3
  1.7 0.1 dynamic_slice.3
  1.8 0.1 and_bitcast_fusion
  1.9 0.7 copy.20.masks_ref
  2.6 241.1 %hyena_backward.1 = (bf16[3,128,4096]{2,1,0:T(8,128)(2,1)}, f32[16,4096]{1,0:T(8,128)}, f32[4,128,128]{2,1,0:T(8,128)}, f32[3,3,4096]{2,1,0:T(4,128)}) custom-call(bf16[128,4096]{1,0:T(8,128)(2,1)} %grad.1, bf16[2,4,64,4096]{3,2,1,0:T(8,128)(2,1)} %bitcast.11, f32[4,128,128]{2,1,0:T(8,128)} %bitcast.12, bf16[3,128,4096]{2,1,0:T(8,128)(2,1)} %streams.1, ...), custom_call_target="tpu_custom_call" | custom-call | flops 1000000 | bytes 16777216 | tf_op jit(solution)/shard_map/hyena_backward/pallas_call | solution.py:311
  243.8 0.0 copy-start.1
  243.8 0.0 copy-start
  243.8 0.0 copy-start.2
  243.8 4.0 %copy.25 = bf16[3,128,4096]{2,1,0:T(8,128)(2,1)} copy(bf16[3,128,4096]{2,1,0:T(8,128)(2,1)} %get-tuple-element.20) | data formatting | bytes 6291456
  247.8 0.0 copy-done.1
  247.8 0.7 copy.26
  248.5 0.0 copy-done
  248.5 0.7 copy.27
  249.2 0.0 copy-done.2
  249.2 0.7 copy.28
  (4 shorter events, 0.0 us)
Async XLA Ops:
  243.8 4.0 %copy-start.1 = (f32[16,4096]{1,0:T(8,128)S(1)}, f32[16,4096]{1,0:T(8,128)}, u32[]{:S(2)}) copy-start(f32[16,4096]{1,0:T(8,128)} %get-tuple-element.21) | copy-start | bytes 786436
  243.8 4.7 %copy-start = (f32[4,128,128]{2,1,0:T(8,128)S(1)}, f32[4,128,128]{2,1,0:T(8,128)}, u32[]{:S(2)}) copy-start(f32[4,128,128]{2,1,0:T(8,128)} %get-tuple-element.10) | copy-start | bytes 786436
  243.8 5.4 %copy-start.2 = (f32[3,3,4096]{2,1,0:T(4,128)S(1)}, f32[3,3,4096]{2,1,0:T(4,128)}, u32[]{:S(2)}) copy-start(f32[3,3,4096]{2,1,0:T(4,128)} %get-tuple-element.23) | copy-start | bytes 442372
